TPU v7x, 512 devices: a whole 4x8x8 slice. The times are simulated.
512 devices in a mesh: gx: 8 (over z), gy: 64 (over x, y, core).
Axes of the slice: x: 4, y: 8, z: 8, core: 2. Of those that a mesh axis runs over, the one named last changes fastest.
Arguments:
- features: bfloat16 [1024, 512, 128], P(('gx', 'gy')), may hold values from -6 to 6
- occupancy: int32 [1024, 512], P(('gx', 'gy')), may hold values 0 or 1
- weights: bfloat16 [7, 128, 128], replicated, may hold values from -0.1875 to 0.1875
- cotangent: bfloat16 [1024, 512, 128], P(('gx', 'gy')), may hold values from -6 to 6
- send_count: int32 [512, 64], P(('gx', 'gy')), may hold values from 0 to 1, as said below
- send_face: int32 [512, 64, 1], P(('gx', 'gy')), may hold values from 0 to 11, as said below
- recv_face: int32 [512, 64, 1], P(('gx', 'gy')), may hold values from -1 to 11, as said below
Outputs:
- activated: bfloat16 [1024, 512, 128], P(('gx', 'gy'))
- feature_grad: bfloat16 [1024, 512, 128], P(('gx', 'gy'))
- weight_grad: float32 [7, 128, 128], replicated
Inputs may be any that keep to these rules, and one draw needn't show every extreme that they name: `send_count`: at most 1 faces go from one device to one peer, and every device receives 1 faces from some peer. `send_face`: side is the opposite of the side that the receiving slot fills; entries of slots beyond send_count are arbitrary valid faces. `recv_face`: slot s from peer p is used exactly when s < that peer's send_count to this device; the used slots of one device fill distinct ghost faces.
All inputs are finite; a program needn't handle non-finite values. No bound on the sum of `occupancy` on one device may be relied on, other than what follows from the above.
Results may differ from a plain program's by a relative error of at most 0.0049.
Values may be sent and summed in bfloat16 or wider, within the bound.
A program may use at most 64 MiB of HBM per device.

v0:
```python
import jax
import jax.numpy as jnp
from jax import lax
from jax.sharding import PartitionSpec as P

tap_starts = ((1, 1, 1), (0, 1, 1), (2, 1, 1), (1, 0, 1), (1, 2, 1), (1, 1, 0), (1, 1, 2))


def side_faces(cube):
    bricks = cube.shape[0]
    width = cube.shape[-1]
    planes = [
        cube[:, 0],
        cube[:, 7],
        cube[:, :, 0],
        cube[:, :, 7],
        cube[:, :, :, 0],
        cube[:, :, :, 7],
    ]
    return jnp.stack([plane.reshape(bricks, 64 * width) for plane in planes], axis=1)


def padded_cube(cube, ghost):
    bricks = cube.shape[0]
    width = cube.shape[-1]
    planes = ghost.reshape(bricks, 6, 8, 8, width)
    padded = jnp.pad(cube, ((0, 0), (1, 1), (1, 1), (1, 1), (0, 0)))
    padded = padded.at[:, 0, 1:9, 1:9].set(planes[:, 0])
    padded = padded.at[:, 9, 1:9, 1:9].set(planes[:, 1])
    padded = padded.at[:, 1:9, 0, 1:9].set(planes[:, 2])
    padded = padded.at[:, 1:9, 9, 1:9].set(planes[:, 3])
    padded = padded.at[:, 1:9, 1:9, 0].set(planes[:, 4])
    padded = padded.at[:, 1:9, 1:9, 9].set(planes[:, 5])
    return padded


def tap_views(padded):
    return [padded[:, sx : sx + 8, sy : sy + 8, sz : sz + 8] for sx, sy, sz in tap_starts]


def convolve(views, weights):
    width = weights.shape[-1]
    total = jnp.zeros((views[0].size // width, width), jnp.float32)
    for tap_index in range(7):
        total = total + jnp.dot(
            views[tap_index].reshape(-1, width),
            weights[tap_index],
            preferred_element_type=jnp.float32,
        )
    return total.reshape(views[0].shape)


def add_layers(cube, planes):
    cube = cube.at[:, 0].add(planes[:, 0])
    cube = cube.at[:, 7].add(planes[:, 1])
    cube = cube.at[:, :, 0].add(planes[:, 2])
    cube = cube.at[:, :, 7].add(planes[:, 3])
    cube = cube.at[:, :, :, 0].add(planes[:, 4])
    cube = cube.at[:, :, :, 7].add(planes[:, 5])
    return cube


def place_ghosts(received, recv_rows, face_total):
    group, slots, flat = received.shape
    flat_rows = recv_rows.reshape(-1)
    target = jnp.where(flat_rows >= 0, flat_rows, face_total)
    source_slot = (
        jnp.full((face_total + 1,), group * slots, jnp.int32)
        .at[target]
        .set(jnp.arange(group * slots, dtype=jnp.int32))
    )
    stacked = jnp.concatenate(
        [received.reshape(group * slots, flat), jnp.zeros((1, flat), received.dtype)], axis=0
    )
    return stacked[source_slot[:face_total]]


def transpose_conv(delta, weights):
    bricks = delta.shape[0]
    width = weights.shape[-1]
    flat_delta = delta.reshape(-1, width)
    grad_pad = jnp.zeros((bricks, 10, 10, 10, width), jnp.float32)
    for tap_index in range(7):
        sx, sy, sz = tap_starts[tap_index]
        product = lax.dot_general(
            flat_delta,
            weights[tap_index],
            (((1,), (1,)), ((), ())),
            preferred_element_type=jnp.float32,
        )
        grad_pad = grad_pad.at[:, sx : sx + 8, sy : sy + 8, sz : sz + 8].add(
            product.reshape(delta.shape)
        )
    return grad_pad[:, 1:9, 1:9, 1:9]


def face_gradients(back, send_rows, send_counts, weights, face_total):
    group, slots, flat = back.shape
    width = weights.shape[-1]
    valid = jnp.arange(slots, dtype=jnp.int32)[None, :] < send_counts[:, None]
    sides = send_rows % 6
    taps = 1 + sides + 1 - 2 * (sides % 2)
    chosen = weights[taps.reshape(-1)]
    contrib = jnp.einsum(
        "sfd,scd->sfc",
        back.reshape(group * slots, 64, width),
        chosen,
        preferred_element_type=jnp.float32,
    )
    contrib = jnp.where(valid.reshape(-1, 1, 1), contrib, jnp.zeros_like(contrib))
    target = jnp.where(valid, send_rows, face_total).reshape(-1)
    summed = jnp.zeros((face_total + 1, 64, width), jnp.float32).at[target].add(contrib)
    return summed[:face_total]


def on_device(features, occupancy, weights, cotangent, send_count, send_face, recv_face):
    brick_count = features.shape[0]
    width = features.shape[2]
    face_total = brick_count * 6
    occupied = (occupancy > 0)[..., None]
    masked = jnp.where(occupied, features, jnp.zeros_like(features))
    cube = masked.reshape(brick_count, 8, 8, 8, width)
    mask_cube = occupied.astype(jnp.float32).reshape(brick_count, 8, 8, 8, 1)
    own_faces = side_faces(cube).reshape(face_total, 64 * width)
    counts = send_count[0]
    sent_rows = send_face[0]
    recv_rows = recv_face[0]
    slots = sent_rows.shape[1]
    valid = jnp.arange(slots, dtype=jnp.int32)[None, :] < counts[:, None]
    picked = own_faces[sent_rows]
    outgoing = jnp.where(valid[..., None], picked, jnp.zeros_like(picked))
    incoming = lax.all_to_all(outgoing, "gy", split_axis=0, concat_axis=0, tiled=True)
    ghost = place_ghosts(incoming, recv_rows, face_total).reshape(brick_count, 6, 64 * width)
    views = tap_views(padded_cube(cube, ghost))
    preact = convolve(views, weights)
    sigma = jax.nn.sigmoid(preact)
    activated = (mask_cube * preact * sigma).astype(jnp.bfloat16)
    cot_cube = cotangent.reshape(brick_count, 8, 8, 8, width).astype(jnp.float32)
    delta = (cot_cube * mask_cube * sigma * (1.0 + preact * (1.0 - sigma))).astype(jnp.bfloat16)
    flat_delta = delta.reshape(-1, width)
    partial_grad = jnp.stack(
        [
            lax.dot_general(
                view.reshape(-1, width),
                flat_delta,
                (((0,), (0,)), ((), ())),
                preferred_element_type=jnp.float32,
            )
            for view in views
        ]
    )
    delta_faces = side_faces(delta).reshape(face_total, 64 * width)
    fetched = delta_faces[jnp.maximum(recv_rows, 0)]
    returned = jnp.where((recv_rows >= 0)[..., None], fetched, jnp.zeros_like(fetched))
    back = lax.all_to_all(returned, "gy", split_axis=0, concat_axis=0, tiled=True)
    inner_grad = transpose_conv(delta, weights)
    extra = face_gradients(back, sent_rows, counts, weights, face_total).reshape(
        brick_count, 6, 8, 8, width
    )
    total_grad = add_layers(inner_grad, extra)
    feature_grad = (mask_cube * total_grad).astype(jnp.bfloat16).reshape(brick_count, 512, width)
    scale = float(lax.axis_size("gx") * lax.axis_size("gy") * brick_count * 512) ** (-0.5)
    summed = lax.psum(partial_grad, ("gx", "gy"))
    weight_grad = summed * scale
    return (activated.reshape(brick_count, 512, width), feature_grad, weight_grad)


def solution(mesh):
    placed = (
        P(("gx", "gy"), None, None),
        P(("gx", "gy"), None),
        P(),
        P(("gx", "gy"), None, None),
        P(("gx", "gy"), None),
        P(("gx", "gy"), None, None),
        P(("gx", "gy"), None, None),
    )
    return jax.shard_map(
        on_device,
        mesh=mesh,
        in_specs=placed,
        out_specs=(P(("gx", "gy"), None, None), P(("gx", "gy"), None, None), P()),
        check_vma=False,
    )
```

profile of v0, /device:TPU:1, one launch (start us, length us, event | category | flops | bytes accessed | tf_op | source)
XLA Modules:
  0.0 387.9 jit_solution(9183933125681028236)
XLA Ops:
  7.2 0.7 convert_bitcast_fusion
  7.9 1.1 broadcast_select_fusion
  9.1 0.3 slice_reduce_fusion
  10.0 1.2 gather_fusion
  11.4 0.5 broadcast.671
  11.9 1.4 reduce.43
  13.3 1.6 reshape.1281
  14.9 11.9 %all-to-all-start = ((bf16[64,2,4096]{2,1,0:T(2,128)(2,1)}), bf16[64,2,4096]{2,1,0:T(2,128)(2,1)}, u32[]{:S(2)}, u32[]{:S(2)}) async-start(bf16[64,2,4096]{2,1,0:T(2,128)(2,1)} %reshape.1281), calls=%async_computation | async-start | bytes 2097152 | tf_op jit(solution)/shard_map/all_to_all | solution.py:132
  27.3 0.9 convert.6
  28.2 2.2 gather_fusion.3
  30.4 1.0 scatter_custom_fusion
  31.4 23.9 %all-to-all-done = bf16[64,2,4096]{2,1,0:T(2,128)(2,1)} async-done(((bf16[64,2,4096]{2,1,0:T(2,128)(2,1)}), bf16[64,2,4096]{2,1,0:T(2,128)(2,1)}, u32[]{:S(2)}, u32[]{:S(2)}) %all-to-all-start) | async-done | bytes 1048608 | tf_op jit(solution)/shard_map/all_to_all | solution.py:132
  55.3 6.5 %reshape.1282 = bf16[64,1,8192]{2,1,0:T(2,128)(2,1)S(1)} reshape(bf16[64,2,4096]{2,1,0:T(2,128)(2,1)} %all-to-all-done) | data formatting | bytes 2097152
  61.8 1.1 copy.199
  63.1 0.7 gather_fusion.1
  64.7 1.4 scatter.42
  66.0 1.4 scatter.43
  67.4 0.4 fusion.72
  68.0 0.2 convolution_add_fusion.11
  68.3 0.2 convolution_add_fusion.10
  68.5 0.2 convolution_add_fusion.9
  68.7 0.2 convolution_add_fusion.8
  68.9 0.2 convolution_add_fusion.7
  69.1 0.5 copy-done.7
  69.7 0.4 fusion.10
  70.1 0.6 copy-done.4
  70.7 0.3 fusion.13
  71.0 0.3 fusion.7
  71.5 0.4 fusion.6
  71.9 0.4 fusion.5
  72.3 0.4 fusion.4
  72.6 0.4 fusion.3
  73.0 0.3 fusion.2
  73.3 0.4 fusion.1
  73.7 0.8 copy-done.5
  75.1 1.2 gather_fusion.2
  76.5 1.4 reduce.44
  77.9 1.6 reshape.1283
  79.5 6.4 %all-to-all-start.1 = ((bf16[64,2,4096]{2,1,0:T(2,128)(2,1)}), bf16[64,2,4096]{2,1,0:T(2,128)(2,1)}, u32[]{:S(2)}, u32[]{:S(2)}) async-start(bf16[64,2,4096]{2,1,0:T(2,128)(2,1)} %reshape.1283), calls=%async_computation.1 | async-start | bytes 2097152 | tf_op jit(solution)/shard_map/all_to_all | solution.py:155
  86.0 0.2 fusion.32
  86.4 0.2 convolution_add_fusion.5
  86.6 2.7 scatter-add.51
  89.3 0.2 convolution_add_fusion.4
  89.6 2.7 scatter-add.54
  92.3 0.2 convolution_add_fusion.3
  92.5 2.7 scatter-add.55
  95.2 0.2 convolution_add_fusion.2
  95.4 2.7 scatter-add.56
  98.1 0.3 fusion
  98.4 0.2 convolution_add_fusion
  98.7 2.7 scatter-add.60
  101.5 0.9 multiply_convert_fusion.1
  102.4 245.7 %all-reduce.5.cloned.1.call-done = f32[7,128,128]{2,1,0:T(8,128)} async-done(((f32[7,128,128]{2,1,0:T(8,128)}), f32[7,128,128]{2,1,0:T(8,128)}) %all-reduce.5.cloned.1.call-update) | async-done | bytes 458768 | tf_op jit(solution)/shard_map/psum | solution.py:163
  348.2 1.8 broadcast_multiply_fusion
  350.0 7.5 %reshape.1284 = bf16[64,1,8192]{2,1,0:T(2,128)(2,1)} reshape(bf16[64,2,4096]{2,1,0:T(2,128)(2,1)} %all-to-all-done.1) | data formatting | bytes 2097152
  357.5 7.9 %reduce.40 = bf16[64,8192]{1,0:T(8,128)(2,1)S(1)} reduce(bf16[64,1,8192]{2,1,0:T(2,128)(2,1)} %reshape.1284, bf16[]{:T(256)} %constant.622), dimensions={1}, to_apply=%all_to_all.7.reduce_sub_computation | reduce | bytes 2097154 | tf_op jit(solution)/shard_map/all_to_all | solution.py:155
  365.4 0.3 copy.173
  365.6 1.3 copy-done.1
  367.0 2.9 convolution_select_fusion
  369.9 7.1 %scatter_fusion = f32[13,64,128]{2,1,0:T(8,128)S(1)} fusion(f32[13,64,128]{2,1,0:T(8,128)S(1)} %broadcast_in_dim.62, s32[64]{0:T(128)S(1)} %get-tuple-element.263, f32[64,64,128]{2,1,0:T(8,128)} %convolution_select_fusion), kind=kCustom, calls=%fused_computation.5 | custom fusion | flops 524288 | bytes 6291712 | tf_op jit(solution)/shard_map/scatter-add | solution.py:112
  377.2 1.3 scatter-add.66
  378.6 1.3 scatter-add.69
  380.0 0.2 multiply_convert_fusion
  380.2 0.9 copy.141
  (101 shorter events, 3.8 us)
Async XLA Ops:
  7.2 2.8 copy-start.8
  7.2 2.8 copy-start.9
  14.9 12.4 %copy-start.6 = (bf16[2,512,128]{2,1,0:T(8,128)(2,1)S(1)}, bf16[2,512,128]{2,1,0:T(8,128)(2,1)}, u32[]{:S(2)}) copy-start(bf16[2,512,128]{2,1,0:T(8,128)(2,1)} %param.48) | copy-start | bytes 786436
  14.9 13.3 %copy-start.10 = (s32[1,64,1]{1,2,0:T(1,128)S(1)}, s32[1,64,1]{1,2,0:T(1,128)}, u32[]{:S(2)}) copy-start(s32[1,64,1]{1,2,0:T(1,128)} %param.51) | copy-start | bytes 772
  14.9 13.3 %copy-start = (bf16[7,128,128]{2,1,0:T(8,128)(2,1)S(1)}, bf16[7,128,128]{2,1,0:T(8,128)(2,1)}, u32[]{:S(2)}) copy-start(bf16[7,128,128]{2,1,0:T(8,128)(2,1)} %param.47) | copy-start | bytes 688132
  14.9 40.4 %all-to-all-start = ((bf16[64,2,4096]{2,1,0:T(2,128)(2,1)}), bf16[64,2,4096]{2,1,0:T(2,128)(2,1)}, u32[]{:S(2)}, u32[]{:S(2)}) async-start(bf16[64,2,4096]{2,1,0:T(2,128)(2,1)} %reshape.1281), calls=%async_computation | async-start | bytes 2097152 | tf_op jit(solution)/shard_map/all_to_all | solution.py:132
  26.9 321.3 %all-reduce.5.cloned.1.call-start = ((), (), s32[]{:S(2)}) async-start(), calls=%async_computation.2 | async-start | bytes 917504 | tf_op jit(solution)/shard_map/psum | solution.py:163
  68.7 1.0 copy-start.7
  69.6 1.0 copy-start.4
  70.0 1.3 copy-start.2
  73.7 0.8 copy-start.5
  79.5 270.4 %all-to-all-start.1 = ((bf16[64,2,4096]{2,1,0:T(2,128)(2,1)}), bf16[64,2,4096]{2,1,0:T(2,128)(2,1)}, u32[]{:S(2)}, u32[]{:S(2)}) async-start(bf16[64,2,4096]{2,1,0:T(2,128)(2,1)} %reshape.1283), calls=%async_computation.1 | async-start | bytes 2097152 | tf_op jit(solution)/shard_map/all_to_all | solution.py:155
  98.6 2.9 copy-start.3
  365.4 1.6 copy-start.1
Sparse Core Ops, SparseCore 0:
  74.6 273.4 all-reduce.4
where the time goes:
time: 389 us; the launch traced here: 388 us
  waiting for transfers between devices  270 us (69%)
  local copies, waits for them, and re-layouts  51.8 us (13%)
  other arithmetic  24.4 us (6%)
  starting transfers between devices  18.4 us (5%)
  between operations  14.9 us (4%)
  matrix products  8.71 us (2%)
    psum x1, waiting for transfers between devices, on_device(): summed = lax.psum(partial_grad, ('gx', 'gy'))  246 us
    all_to_all x1, waiting for transfers between devices, on_device(): lax.all_to_all(outgoing, 'gy', split_axis=0, concat_axis=0, tiled=True)  23.9 us
    unnamed x44, local copies, waits for them, and re-layouts  22.3 us
    scatter-add x6, local copies, waits for them, and re-layouts, transpose_conv(): grad_pad.at[:, sx:sx + 8, sy:sy + 8, sz:sz + 8]  13.6 us
    all_to_all x1, starting transfers between devices, on_device(): lax.all_to_all(outgoing, 'gy', split_axis=0, concat_axis=0, tiled=True)  11.9 us
    all_to_all x1, other arithmetic, on_device(): lax.all_to_all(returned, 'gy', split_axis=0, concat_axis=0, tiled=True)  7.87 us
  transfers between devices with their start and end apart: 3, of which 2 were waited for; matrix products, arithmetic and copies ran while one was open for 7% of the time, Pallas kernels for 0%

commit v1 on v0

v1 whole, which is shorter than its diff:
```python
import functools

import jax
import jax.numpy as jnp
from jax import lax
from jax.experimental import pallas as pl
from jax.experimental.pallas import tpu as pltpu
from jax.sharding import PartitionSpec as P

XN = 4
YN = 8
CN = 2
MESH = pl.DeviceIdType.MESH
CH = 128
NB = 2
FACES = NB * 6
VOX = 512
ROWS = NB * VOX
TAPS = 7
OPPOSITE = (0, 2, 1, 4, 3, 6, 5)
BF = jnp.bfloat16
F32 = jnp.float32


def product(a, b):
    return jnp.dot(a, b, preferred_element_type=F32)


def cut_faces(cube, faces):
    for b in range(NB):
        base = b * VOX
        body = cube[base : base + VOX, :].reshape(8, 8, 8, CH)
        faces[b * 6 + 0] = cube[base : base + 64, :].astype(BF)
        faces[b * 6 + 1] = cube[base + 448 : base + 512, :].astype(BF)
        faces[b * 6 + 2] = body[:, 0].reshape(64, CH).astype(BF)
        faces[b * 6 + 3] = body[:, 7].reshape(64, CH).astype(BF)
        faces[b * 6 + 4] = cube[pl.ds(base, 64, stride=8), :].astype(BF)
        faces[b * 6 + 5] = cube[pl.ds(base + 7, 64, stride=8), :].astype(BF)


def build_views(cube, ghost, shifted, views):
    for b in range(NB):
        base = b * VOX
        rows = slice(base, base + VOX)
        g = b * 6
        body = cube[rows, :]
        solid = body.reshape(8, 8, 8, CH)
        views[rows, 0:128] = body.astype(BF)
        views[base : base + 64, 128:256] = ghost[g + 0].astype(BF)
        views[base + 64 : base + 512, 128:256] = cube[base : base + 448, :].astype(BF)
        views[base : base + 448, 256:384] = cube[base + 64 : base + 512, :].astype(BF)
        views[base + 448 : base + 512, 256:384] = ghost[g + 1].astype(BF)
        low = ghost[g + 2].reshape(8, 1, 8, CH)
        high = ghost[g + 3].reshape(8, 1, 8, CH)
        views[rows, 384:512] = jnp.concatenate([low, solid[:, :7]], axis=1).reshape(VOX, CH).astype(BF)
        views[rows, 512:640] = jnp.concatenate([solid[:, 1:], high], axis=1).reshape(VOX, CH).astype(BF)
        shifted[1:VOX, :] = cube[base : base + VOX - 1, :]
        shifted[pl.ds(0, 64, stride=8), :] = ghost[g + 4]
        views[rows, 640:768] = shifted[...].astype(BF)
        shifted[0 : VOX - 1, :] = cube[base + 1 : base + VOX, :]
        shifted[pl.ds(7, 64, stride=8), :] = ghost[g + 5]
        views[rows, 768:896] = shifted[...].astype(BF)


def kernel(
    zn, gn, scale,
    feat, occ, wcat, cot, count, sface, rface,
    act_out, grad_out, wg_out,
    mask, cube, faces, out1, out2, in1, in2, ghost, shifted, views, wback, delta_t, run, prev,
    part, zsend, zrecv, xsend, xrecv, yrecv, xgath, zgath,
    sems,
):
    z = lax.axis_index("gx")
    me = lax.axis_index("gy")
    xc_n = XN * CN
    my_x = me // (YN * CN)
    my_y = lax.rem(me // CN, YN)
    my_c = lax.rem(me, CN)
    my_xc = my_x * CN + my_c
    share = TAPS * CH // zn
    piece = xsend.shape[1]

    def z_peer(k):
        return lax.rem(z + k, zn)

    def xc_peer(k):
        return lax.rem(my_xc + k, xc_n)

    def xc_device(xc):
        return (xc // CN * YN + my_y) * CN + lax.rem(xc, CN)

    def y_peer(k):
        return lax.rem(my_y + k, YN)

    def y_device(y):
        return (my_x * YN + y) * CN + my_c

    barrier = pltpu.get_barrier_semaphore()

    def greet_group(k, _):
        pl.semaphore_signal(barrier, inc=1, device_id=(z, lax.rem(me + k, gn)), device_id_type=MESH)
        return 0

    def greet_z(k, _):
        pl.semaphore_signal(barrier, inc=1, device_id=(z_peer(k), me), device_id_type=MESH)
        return 0

    lax.fori_loop(1, gn, greet_group, 0)
    lax.fori_loop(1, zn, greet_z, 0)

    diagonal = lax.broadcasted_iota(jnp.int32, (CH, CH), 0) == lax.broadcasted_iota(jnp.int32, (CH, CH), 1)
    ones = jnp.ones((CH, CH), BF)
    for b in range(NB):
        for i in range(VOX // CH):
            row = (occ[b : b + 1, i * CH : (i + 1) * CH] > 0).astype(F32)
            spread = jnp.where(diagonal, jnp.broadcast_to(row, (CH, CH)), 0.0).astype(BF)
            at = b * VOX + i * CH
            flags = product(spread, ones)
            mask[at : at + CH, :] = flags
            cube[at : at + CH, :] = jnp.where(flags > 0, feat[at : at + CH, :].astype(F32), 0.0)
    cut_faces(cube, faces)

    def fill_sent(q, _):
        out1[q] = faces[sface[q]]
        return 0

    lax.fori_loop(0, gn, fill_sent, 0)
    pl.semaphore_wait(barrier, gn - 1 + zn - 1)

    def exchange(out, landed, send_sem, recv_sem):
        def one(k, _):
            q = lax.rem(me + k, gn)
            pltpu.make_async_remote_copy(
                src_ref=out.at[q], dst_ref=landed.at[me], send_sem=send_sem, recv_sem=recv_sem,
                device_id=(z, q), device_id_type=MESH,
            ).start()
            return 0

        lax.fori_loop(1, gn, one, 0)

    def wait_for(ref, sem):
        pltpu.make_async_copy(ref, ref, sem).wait()

    exchange(out1, in1, sems.at[0], sems.at[1])
    in1[me] = out1[me]

    for t in range(TAPS):
        o = OPPOSITE[t]
        wback[t * CH : (t + 1) * CH, :] = wcat[o * CH : (o + 1) * CH, :].astype(F32).T.astype(BF)

    def find_source(p, found):
        row = rface[p]
        return tuple(jnp.where(row == f, p, found[f]) for f in range(FACES))

    source = lax.fori_loop(0, gn, find_source, tuple(jnp.int32(-1) for _ in range(FACES)))

    def chain(q, last):
        face = jnp.where(count[q] > 0, sface[q], FACES)
        before = jnp.int32(0)
        for f in range(FACES):
            before = jnp.where(face == f, last[f], before)
        prev[q] = before
        return tuple(jnp.where(face == f, q + 1, last[f]) for f in range(FACES))

    last = lax.fori_loop(0, gn, chain, tuple(jnp.int32(0) for _ in range(FACES)))

    wait_for(in1.at[pl.ds(0, gn - 1)], sems.at[1])
    for f in range(FACES):
        taken = in1[jnp.maximum(source[f], 0)].astype(F32)
        ghost[f] = jnp.where(source[f] >= 0, taken, 0.0)

    build_views(cube, ghost, shifted, views)
    for b in range(2 * NB):
        rows = slice(b * VOX // 2, (b + 1) * VOX // 2)
        preact = product(views[rows, :], wcat[...])
        sigma = jax.nn.sigmoid(preact)
        flags = mask[rows, :]
        act_out[rows, :] = (flags * preact * sigma).astype(BF)
        delta = (cot[rows, :].astype(F32) * flags * sigma * (1.0 + preact * (1.0 - sigma))).astype(BF)
        cube[rows, :] = delta.astype(F32)
    cut_faces(cube, faces)

    def fill_returned(p, _):
        out2[p] = faces[jnp.maximum(rface[p], 0)]
        return 0

    lax.fori_loop(0, gn, fill_returned, 0)
    exchange(out2, in2, sems.at[2], sems.at[3])
    in2[me] = out2[me]

    delta_t[...] = cube[...].T.astype(BF)
    for t in range(TAPS):
        part[t * CH : (t + 1) * CH, :] = product(delta_t[...], views[:, t * CH : (t + 1) * CH]).T
    zsend[...] = part[...].astype(BF).reshape(zn, share, CH)

    def send_z(out, at_out, landed, send_sem, recv_sem):
        def one(k, _):
            q = z_peer(k)
            pltpu.make_async_remote_copy(
                src_ref=out.at[q] if at_out else out.at[z], dst_ref=landed.at[z], send_sem=send_sem, recv_sem=recv_sem,
                device_id=(q, me), device_id_type=MESH,
            ).start()
            return 0

        lax.fori_loop(1, zn, one, 0)

    def send_xc(out, at_out, landed, send_sem, recv_sem):
        def one(k, _):
            q = xc_peer(k)
            pltpu.make_async_remote_copy(
                src_ref=out.at[q] if at_out else out.at[my_xc], dst_ref=landed.at[my_xc], send_sem=send_sem,
                recv_sem=recv_sem, device_id=(z, xc_device(q)), device_id_type=MESH,
            ).start()
            return 0

        lax.fori_loop(1, xc_n, one, 0)

    send_z(zsend, True, zrecv, sems.at[4], sems.at[5])
    zrecv[z] = jnp.zeros((share, CH), BF)
    own = part[pl.ds(pl.multiple_of(z * share, 16), share), :]
    wait_for(zrecv.at[pl.ds(0, zn - 1)], sems.at[5])
    total = own
    for k in range(zn):
        total = total + zrecv[k].astype(F32)
    padding = jnp.zeros((piece * xc_n - share, CH), F32)
    xsend[...] = jnp.concatenate([total, padding], axis=0).reshape(xc_n, piece, CH)
    send_xc(xsend, True, xrecv, sems.at[6], sems.at[7])
    xrecv[my_xc] = xsend[my_xc]
    wait_for(xrecv.at[pl.ds(0, xc_n - 1)], sems.at[7])
    total = xrecv[0]
    for k in range(1, xc_n):
        total = total + xrecv[k]
    yrecv[my_y] = total

    def send_y(k, _):
        pltpu.make_async_remote_copy(
            src_ref=yrecv.at[my_y], dst_ref=yrecv.at[my_y], send_sem=sems.at[8], recv_sem=sems.at[9],
            device_id=(z, y_device(y_peer(k))), device_id_type=MESH,
        ).start()
        return 0

    lax.fori_loop(1, YN, send_y, 0)
    wait_for(yrecv.at[pl.ds(0, YN - 1)], sems.at[9])
    total = yrecv[0]
    for k in range(1, YN):
        total = total + yrecv[k]
    xgath[my_xc] = total.astype(BF)
    send_xc(xgath, False, xgath, sems.at[10], sems.at[11])
    wait_for(xgath.at[pl.ds(0, xc_n - 1)], sems.at[11])
    zgath[z] = xgath[...].reshape(xc_n * piece, CH)[:share]
    send_z(zgath, False, zgath, sems.at[12], sems.at[13])
    wait_for(zgath.at[pl.ds(0, zn - 1)], sems.at[13])
    wg_out[...] = zgath[...].reshape(TAPS * CH, CH).astype(F32) * scale

    wait_for(in2.at[pl.ds(0, gn - 1)], sems.at[3])
    run[0] = jnp.zeros((64, CH), F32)

    def add_up(q, _):
        run[q + 1] = run[prev[q]] + in2[q].astype(F32)
        return 0

    lax.fori_loop(0, gn, add_up, 0)
    for f in range(FACES):
        ghost[f] = run[last[f]]
    build_views(cube, ghost, shifted, views)
    for b in range(2 * NB):
        rows = slice(b * VOX // 2, (b + 1) * VOX // 2)
        grad = product(views[rows, :], wback[...])
        grad_out[rows, :] = (mask[rows, :] * grad).astype(BF)

    wait_for(out1.at[pl.ds(0, gn - 1)], sems.at[0])
    wait_for(out2.at[pl.ds(0, gn - 1)], sems.at[2])
    wait_for(zsend.at[pl.ds(0, zn - 1)], sems.at[4])
    wait_for(xsend.at[pl.ds(0, xc_n - 1)], sems.at[6])
    wait_for(yrecv.at[pl.ds(0, YN - 1)], sems.at[8])
    wait_for(xgath.at[pl.ds(0, xc_n - 1)], sems.at[10])
    wait_for(zgath.at[pl.ds(0, zn - 1)], sems.at[12])


def on_device(zn, gn, features, occupancy, weights, cotangent, send_count, send_face, recv_face):
    vmem = pl.BlockSpec(memory_space=pltpu.VMEM)
    smem = pl.BlockSpec(memory_space=pltpu.SMEM)
    xc_n = XN * CN
    share = TAPS * CH // zn
    piece = -(-share // (16 * xc_n)) * 16
    scale = float(zn * gn * ROWS) ** (-0.5)
    activated, grad, weight_grad = pl.pallas_call(
        functools.partial(kernel, zn, gn, scale),
        out_shape=(
            jax.ShapeDtypeStruct((ROWS, CH), BF),
            jax.ShapeDtypeStruct((ROWS, CH), BF),
            jax.ShapeDtypeStruct((TAPS * CH, CH), F32),
        ),
        in_specs=[vmem, vmem, vmem, vmem, smem, smem, smem],
        out_specs=(vmem, vmem, vmem),
        scratch_shapes=[
            pltpu.VMEM((ROWS, CH), F32),
            pltpu.VMEM((ROWS, CH), F32),
            pltpu.VMEM((FACES, 64, CH), BF),
            pltpu.VMEM((gn, 64, CH), BF),
            pltpu.VMEM((gn, 64, CH), BF),
            pltpu.VMEM((gn, 64, CH), BF),
            pltpu.VMEM((gn, 64, CH), BF),
            pltpu.VMEM((FACES, 64, CH), F32),
            pltpu.VMEM((VOX, CH), F32),
            pltpu.VMEM((ROWS, TAPS * CH), BF),
            pltpu.VMEM((TAPS * CH, CH), BF),
            pltpu.VMEM((CH, ROWS), BF),
            pltpu.VMEM((gn + 1, 64, CH), F32),
            pltpu.SMEM((gn,), jnp.int32),
            pltpu.VMEM((TAPS * CH, CH), F32),
            pltpu.VMEM((zn, share, CH), BF),
            pltpu.VMEM((zn, share, CH), BF),
            pltpu.VMEM((xc_n, piece, CH), F32),
            pltpu.VMEM((xc_n, piece, CH), F32),
            pltpu.VMEM((YN, piece, CH), F32),
            pltpu.VMEM((xc_n, piece, CH), BF),
            pltpu.VMEM((zn, share, CH), BF),
            pltpu.SemaphoreType.DMA((14,)),
        ],
        compiler_params=pltpu.CompilerParams(
            collective_id=0, has_side_effects=True, vmem_limit_bytes=40 * 1024 * 1024
        ),
        cost_estimate=pl.CostEstimate(
            flops=6 * ROWS * TAPS * CH * CH, bytes_accessed=2000000, transcendentals=ROWS * CH
        ),
    )(
        features.reshape(ROWS, CH),
        occupancy,
        weights.reshape(TAPS * CH, CH),
        cotangent.reshape(ROWS, CH),
        send_count.reshape(gn),
        send_face.reshape(gn),
        recv_face.reshape(gn),
    )
    return (
        activated.reshape(NB, VOX, CH),
        grad.reshape(NB, VOX, CH),
        weight_grad.reshape(TAPS, CH, CH),
    )


def solution(mesh):
    zn, gn = mesh.shape["gx"], mesh.shape["gy"]
    split = P(("gx", "gy"), None, None)
    return jax.shard_map(
        functools.partial(on_device, zn, gn),
        mesh=mesh,
        in_specs=(split, P(("gx", "gy"), None), P(), split, P(("gx", "gy"), None), split, split),
        out_specs=(split, split, P()),
        check_vma=False,
    )
```

time: 389 us -> 91.9 us (0.24)
  waiting for transfers between devices: 270 us -> 0 us
  Pallas kernels: 0 us -> 85.3 us
  local copies, waits for them, and re-layouts: 51.8 us -> 5.68 us
  other arithmetic: 24.4 us -> 0 us
  starting transfers between devices: 18.4 us -> 0 us
  between operations: 14.9 us -> 0.68 us
  matrix products: 8.71 us -> 0 us
    psum x1 -> x0, waiting for transfers between devices: 246 us -> none  [on_device(): summed = lax.psum(partial_grad, ('gx', 'gy'))]
    pallas_call x0 -> x1, Pallas kernels: none -> 85.3 us  [on_device(): pl.pallas_call(functools.partial(kernel, zn, gn, scale), out_shape=(jax.S...]
    all_to_all x2 -> x0, waiting for transfers between devices: 23.9 us -> none  [the longest x1 23.9 us: on_device(): lax.all_to_all(outgoing, 'gy', split_axis=0, concat_axis=0, tiled=True)]
    all_to_all x2 -> x0, starting transfers between devices: 18.4 us -> none  [the longest x1 11.9 us: on_device(): lax.all_to_all(outgoing, 'gy', split_axis=0, concat_axis=0, tiled=True)]
    unnamed x44 -> x17, local copies, waits for them, and re-layouts: 22.3 us -> 5.68 us
    scatter-add x9 -> x0, local copies, waits for them, and re-layouts: 16.2 us -> none  [the longest x6 13.6 us: transpose_conv(): grad_pad.at[:, sx:sx + 8, sy:sy + 8, sz:sz + 8]]
    dot_general x22 -> x0, matrix products: 8.71 us -> none  [the longest x1 2.89 us: face_gradients(): jnp.einsum('sfd,scd->sfc', back.reshape(group * slots, 64, width), chosen...]
    all_to_all x1 -> x0, other arithmetic: 7.87 us -> none  [on_device(): lax.all_to_all(returned, 'gy', split_axis=0, concat_axis=0, tiled=True)]
  transfers between devices with their start and end apart: 3 -> 0, of which waited for: 2 -> 0; matrix products, arithmetic and copies ran while one was open for 7% -> 0% of each run, Pallas kernels for 0% -> 0%
where the time goes in v1:
time: 91.9 us; the launch traced here: 91.6 us
  Pallas kernels  85.3 us (93%)
  local copies, waits for them, and re-layouts  5.68 us (6%)
    pallas_call x1, Pallas kernels, on_device(): pl.pallas_call(functools.partial(kernel, zn, gn, scale), out_shape=(jax.S...  85.3 us
    unnamed x17, local copies, waits for them, and re-layouts  5.68 us

profile of v1, /device:TPU:1, one launch (start us, length us, event | category | flops | bytes accessed | tf_op | source)
XLA Modules:
  0.0 91.6 jit_solution(11867239706785838933)
XLA Ops:
  0.6 0.0 copy-start.3
  0.6 0.0 copy-start.4
  0.7 0.0 copy-start.5
  0.7 0.0 copy-start.6
  0.7 0.6 copy-done.3
  1.3 0.0 copy-done.4
  1.3 0.0 copy-done.5
  1.3 0.0 copy-done.6
  1.3 0.0 copy-start
  1.3 0.9 %copy-done = bf16[2,512,128]{2,1,0:T(8,128)(2,1)S(1)} copy-done((bf16[2,512,128]{2,1,0:T(8,128)(2,1)S(1)}, bf16[2,512,128]{2,1,0:T(8,128)(2,1)}, u32[]{:S(2)}) %copy-start) | copy-done | bytes 262168
  2.3 0.0 copy-start.1
  2.3 0.9 %copy-done.1 = bf16[2,512,128]{2,1,0:T(8,128)(2,1)S(1)} copy-done((bf16[2,512,128]{2,1,0:T(8,128)(2,1)S(1)}, bf16[2,512,128]{2,1,0:T(8,128)(2,1)}, u32[]{:S(2)}) %copy-start.1) | copy-done | bytes 262168
  3.2 0.0 copy-start.2
  3.2 0.9 %copy-done.2 = bf16[7,128,128]{2,1,0:T(8,128)(2,1)S(1)} copy-done((bf16[7,128,128]{2,1,0:T(8,128)(2,1)S(1)}, bf16[7,128,128]{2,1,0:T(8,128)(2,1)}, u32[]{:S(2)}) %copy-start.2) | copy-done | bytes 229400
  4.2 85.3 %shard_map.94 = (bf16[1024,128]{1,0:T(8,128)(2,1)S(1)}, bf16[1024,128]{1,0:T(8,128)(2,1)S(1)}, f32[896,128]{1,0:T(8,128)S(1)}) custom-call(bf16[1024,128]{1,0:T(8,128)(2,1)S(1)} %bitcast.12, s32[2,512]{1,0:T(2,128)S(1)} %copy-done.3, bf16[896,128]{1,0:T(8,128)(2,1)S(1)} %bitcast.14, bf16[1024,128]{1,0:T(8,128)(2,1)S(1)} %bitcast.13, s32[64]{0:T(128)S(1)} %bitcast.15, ...), custom_call_target="tpu_custom_call" | custom-call | flops 704643072 | bytes 2000000 | tf_op jit(solution)/shard_map/pallas_call | solution.py:287
  89.4 0.7 copy.13
  90.2 0.7 copy.14
  90.9 0.8 copy.15
Async XLA Ops:
  0.6 0.7 copy-start.3
  0.6 0.7 copy-start.4
  0.7 0.7 copy-start.5
  0.7 0.7 copy-start.6
  1.3 0.9 %copy-start = (bf16[2,512,128]{2,1,0:T(8,128)(2,1)S(1)}, bf16[2,512,128]{2,1,0:T(8,128)(2,1)}, u32[]{:S(2)}) copy-start(bf16[2,512,128]{2,1,0:T(8,128)(2,1)} %param.7) | copy-start | bytes 786436
  2.3 0.9 %copy-start.1 = (bf16[2,512,128]{2,1,0:T(8,128)(2,1)S(1)}, bf16[2,512,128]{2,1,0:T(8,128)(2,1)}, u32[]{:S(2)}) copy-start(bf16[2,512,128]{2,1,0:T(8,128)(2,1)} %param.10) | copy-start | bytes 786436
  3.2 0.9 %copy-start.2 = (bf16[7,128,128]{2,1,0:T(8,128)(2,1)S(1)}, bf16[7,128,128]{2,1,0:T(8,128)(2,1)}, u32[]{:S(2)}) copy-start(bf16[7,128,128]{2,1,0:T(8,128)(2,1)} %param.9) | copy-start | bytes 688132

commit v2 on v1

v2 whole, which is shorter than its diff:
```python
import functools

import jax
import jax.numpy as jnp
from jax import lax
from jax.experimental import pallas as pl
from jax.experimental.pallas import tpu as pltpu
from jax.sharding import PartitionSpec as P

XN = 4
YN = 8
CN = 2
MESH = pl.DeviceIdType.MESH
CH = 128
NB = 2
FACES = NB * 6
VOX = 512
ROWS = NB * VOX
TAPS = 7
OPPOSITE = (0, 2, 1, 4, 3, 6, 5)
BF = jnp.bfloat16
F32 = jnp.float32


def product(a, b):
    return jnp.dot(a, b, preferred_element_type=F32)


def cut_faces(cube, faces):
    for b in range(NB):
        base = b * VOX
        body = cube[base : base + VOX, :].reshape(8, 8, 8, CH)
        faces[b * 6 + 0] = cube[base : base + 64, :].astype(BF)
        faces[b * 6 + 1] = cube[base + 448 : base + 512, :].astype(BF)
        faces[b * 6 + 2] = body[:, 0].reshape(64, CH).astype(BF)
        faces[b * 6 + 3] = body[:, 7].reshape(64, CH).astype(BF)
        faces[b * 6 + 4] = cube[pl.ds(base, 64, stride=8), :].astype(BF)
        faces[b * 6 + 5] = cube[pl.ds(base + 7, 64, stride=8), :].astype(BF)


def build_views(cube, ghost, shifted, views):
    for b in range(NB):
        base = b * VOX
        rows = slice(base, base + VOX)
        g = b * 6
        body = cube[rows, :]
        solid = body.reshape(8, 8, 8, CH)
        views[rows, 0:128] = body.astype(BF)
        views[base : base + 64, 128:256] = ghost[g + 0].astype(BF)
        views[base + 64 : base + 512, 128:256] = cube[base : base + 448, :].astype(BF)
        views[base : base + 448, 256:384] = cube[base + 64 : base + 512, :].astype(BF)
        views[base + 448 : base + 512, 256:384] = ghost[g + 1].astype(BF)
        low = ghost[g + 2].reshape(8, 1, 8, CH)
        high = ghost[g + 3].reshape(8, 1, 8, CH)
        views[rows, 384:512] = jnp.concatenate([low, solid[:, :7]], axis=1).reshape(VOX, CH).astype(BF)
        views[rows, 512:640] = jnp.concatenate([solid[:, 1:], high], axis=1).reshape(VOX, CH).astype(BF)
        shifted[1:VOX, :] = cube[base : base + VOX - 1, :]
        shifted[pl.ds(0, 64, stride=8), :] = ghost[g + 4]
        views[rows, 640:768] = shifted[...].astype(BF)
        shifted[0 : VOX - 1, :] = cube[base + 1 : base + VOX, :]
        shifted[pl.ds(7, 64, stride=8), :] = ghost[g + 5]
        views[rows, 768:896] = shifted[...].astype(BF)


ROW_OF = (0, 4, -1, 1, -2, 2, -3, 3)
PIECES = 3


def kernel(
    zn, gn, scale,
    feat_in, occ_in, wcat_in, cot_in, count_in, sface_in, rface_in,
    act_out, grad_out, wg_out,
    feat, occ, wcat, cot, count, sface, rface,
    mask, cube, ghost, shifted, views, wback, delta_t, run, prev, slot_face, slot_row, meta_out, meta_in,
    faces_a, faces_b, rows_a, rows_b, got_a, got_b, up_a, down_a, up_b, down_b,
    csend, crecv, zsend, zrecv, xgot, ygot, zgath, cgath,
    load_sems, chain_a, chain_b, sems,
):
    z = lax.axis_index("gx")
    me = lax.axis_index("gy")
    xc_n = XN * CN
    my_x = me // (YN * CN)
    my_y = lax.rem(me // CN, YN)
    my_c = lax.rem(me, CN)
    my_xc = my_x * CN + my_c
    half = TAPS * CH // CN
    share = half // zn

    def wrap_y(offset):
        return lax.rem(my_y + offset + YN, YN)

    def at(xc, y):
        return (xc // CN * YN + y) * CN + lax.rem(xc, CN)

    def xc_peer(k):
        return lax.rem(my_xc + k, xc_n)

    def z_peer(k):
        return lax.rem(z + k, zn)

    def repeat(low, high, body):
        def step(i, _):
            body(i)
            return 0

        lax.fori_loop(low, high, step, 0)

    def send(src, dst, send_sem, recv_sem, to):
        copy = pltpu.make_async_remote_copy(
            src_ref=src, dst_ref=dst, send_sem=send_sem, recv_sem=recv_sem, device_id=to, device_id_type=MESH
        )
        copy.start()

    def wait_for(ref, sem):
        pltpu.make_async_copy(ref, ref, sem).wait()

    barrier = pltpu.get_barrier_semaphore()

    def greet(to):
        pl.semaphore_signal(barrier, inc=1, device_id=to, device_id_type=MESH)

    repeat(1, YN, lambda k: greet((z, at(my_xc, wrap_y(k)))))
    repeat(1, xc_n, lambda k: greet((z, at(xc_peer(k), my_y))))
    repeat(1, xc_n, lambda k: greet((z, at(xc_peer(k), wrap_y(4)))))
    if zn > 1:
        repeat(1, zn, lambda k: greet((z_peer(k), me)))

    loads = [
        pltpu.make_async_copy(src, dst, load_sems.at[i])
        for i, (src, dst) in enumerate(
            [(occ_in, occ), (feat_in, feat), (sface_in, sface), (rface_in, rface), (count_in, count), (wcat_in, wcat),
             (cot_in, cot)]
        )
    ]
    for load in loads:
        load.start()

    diagonal = lax.broadcasted_iota(jnp.int32, (CH, CH), 0) == lax.broadcasted_iota(jnp.int32, (CH, CH), 1)
    ones = jnp.ones((CH, CH), BF)
    loads[0].wait()
    loads[1].wait()
    for b in range(NB):
        for i in range(VOX // CH):
            row = (occ[b : b + 1, i * CH : (i + 1) * CH] > 0).astype(F32)
            spread = jnp.where(diagonal, jnp.broadcast_to(row, (CH, CH)), 0.0).astype(BF)
            place = b * VOX + i * CH
            flags = product(spread, ones)
            mask[place : place + CH, :] = flags
            cube[place : place + CH, :] = jnp.where(flags > 0, feat[place : place + CH, :].astype(F32), 0.0)
    cut_faces(cube, faces_a)
    loads[2].wait()
    loads[3].wait()
    loads[4].wait()

    def fill_meta(y):
        for xc in range(xc_n):
            meta_out[y, xc] = sface[at(jnp.int32(xc), y)]
            meta_out[y, xc_n + xc] = jnp.maximum(rface[at(jnp.int32(xc), y)], 0)

    repeat(0, YN, fill_meta)

    def start_exchange(faces, column, rows, got, up, down, chain, row_sems):
        for p in range(PIECES):
            part = pl.ds(p * 4, 4)
            send(faces.at[part], up[0].at[part], chain.at[0], chain.at[6 + p], (z, at(my_xc, wrap_y(1))))
            send(faces.at[part], down[0].at[part], chain.at[3], chain.at[6 + 9 + p], (z, at(my_xc, wrap_y(-1))))
        far = wrap_y(4)

        def pick(xc):
            rows[xc, 0] = faces[meta_out[my_y, column + xc]]
            rows[xc, 1] = faces[meta_out[far, column + xc]]

        repeat(0, xc_n, pick)

        def ship(k):
            xc = xc_peer(k)
            send(rows.at[xc, 1], got.at[my_xc, 1], row_sems.at[0], row_sems.at[1], (z, at(xc, far)))

        repeat(0, xc_n, ship)

        def ship_own(k):
            xc = xc_peer(k)
            send(rows.at[xc, 0], got.at[my_xc, 0], row_sems.at[0], row_sems.at[1], (z, at(xc, my_y)))

        repeat(1, xc_n, ship_own)
        got[my_xc, 0] = rows[my_xc, 0]

    def step_exchange(d, column, rows, got, up, down, chain, row_sems):
        for p in range(PIECES):
            part = pl.ds(p * 4, 4)
            wait_for(up[d - 1].at[part], chain.at[6 + (d - 1) * 3 + p])
            if d < 3:
                send(up[d - 1].at[part], up[d].at[part], chain.at[d], chain.at[6 + d * 3 + p],
                     (z, at(my_xc, wrap_y(1))))
            wait_for(down[d - 1].at[part], chain.at[6 + 9 + (d - 1) * 3 + p])
            if d < 3:
                send(down[d - 1].at[part], down[d].at[part], chain.at[3 + d], chain.at[6 + 9 + d * 3 + p],
                     (z, at(my_xc, wrap_y(-1))))
        low, high = wrap_y(-d), wrap_y(d)

        def pick(xc):
            rows[xc, 2 * d] = up[d - 1][meta_in[low, column + xc]]
            rows[xc, 2 * d + 1] = down[d - 1][meta_in[high, column + xc]]

        repeat(0, xc_n, pick)
        pair = pl.ds(2 * d, 2)

        def ship(k):
            xc = xc_peer(k)
            send(rows.at[xc, pair], got.at[my_xc, pair], row_sems.at[0], row_sems.at[1], (z, at(xc, my_y)))

        repeat(1, xc_n, ship)
        got[my_xc, pair] = rows[my_xc, pair]

    remote_faces = (xc_n - 1) * 7 + xc_n

    def flat(ref):
        return ref.reshape(xc_n * 8, 64, CH).at[pl.ds(0, remote_faces)]

    def drain(rows, up, down, chain, row_sems):
        for d in range(3):
            wait_for(up[d], chain.at[d])
            wait_for(down[d], chain.at[3 + d])
        wait_for(flat(rows), row_sems.at[0])

    pl.semaphore_wait(barrier, (YN - 1) + 2 * (xc_n - 1) + (zn - 1))
    sems_a, sems_b = sems.at[pl.ds(0, 2)], sems.at[pl.ds(2, 2)]
    for d in (1, -1, 2, -2, 3, -3):
        y = wrap_y(d)
        send(meta_out.at[y], meta_in.at[my_y], sems.at[4], sems.at[5], (z, at(my_xc, y)))
    first = (rows_a, got_a, up_a, down_a, chain_a, sems_a)
    second = (rows_b, got_b, up_b, down_b, chain_b, sems_b)
    start_exchange(faces_a, 0, *first)

    def list_slots(xc):
        for s in range(8):
            p = at(xc, wrap_y(ROW_OF[s]))
            slot_row[xc * 8 + s] = rface[p]
            slot_face[xc * 8 + s] = jnp.where(count[p] > 0, sface[p], FACES)

    repeat(0, xc_n, list_slots)

    def find_source(j, found):
        row = slot_row[j]
        return tuple(jnp.where(row == f, j, found[f]) for f in range(FACES))

    source = lax.fori_loop(0, gn, find_source, tuple(jnp.int32(-1) for _ in range(FACES)))
    loads[5].wait()
    loads[6].wait()
    wait_for(meta_in.at[pl.ds(0, 6)], sems.at[5])
    step_exchange(1, 0, *first)
    for t in range(TAPS):
        o = OPPOSITE[t]
        wback[t * CH : (t + 1) * CH, :] = wcat[o * CH : (o + 1) * CH, :].astype(F32).T.astype(BF)
    step_exchange(2, 0, *first)

    def chain_up(j, last):
        face = slot_face[j]
        before = jnp.int32(0)
        for f in range(FACES):
            before = jnp.where(face == f, last[f], before)
        prev[j] = before
        return tuple(jnp.where(face == f, j + 1, last[f]) for f in range(FACES))

    last = lax.fori_loop(0, gn, chain_up, tuple(jnp.int32(0) for _ in range(FACES)))
    step_exchange(3, 0, *first)

    wait_for(flat(got_a), sems_a.at[1])
    for f in range(FACES):
        j = jnp.maximum(source[f], 0)
        taken = got_a[j // 8, lax.rem(j, 8)].astype(F32)
        ghost[f] = jnp.where(source[f] >= 0, taken, 0.0)

    build_views(cube, ghost, shifted, views)
    for b in range(2 * NB):
        rows = slice(b * VOX // 2, (b + 1) * VOX // 2)
        preact = product(views[rows, :], wcat[...])
        sigma = jax.nn.sigmoid(preact)
        flags = mask[rows, :]
        act_out[rows, :] = (flags * preact * sigma).astype(BF)
        delta = (cot[rows, :].astype(F32) * flags * sigma * (1.0 + preact * (1.0 - sigma))).astype(BF)
        cube[rows, :] = delta.astype(F32)
    cut_faces(cube, faces_b)
    start_exchange(faces_b, xc_n, *second)

    delta_t[...] = cube[...].T.astype(BF)
    for t in range(TAPS):
        csend[t * CH : (t + 1) * CH, :] = product(delta_t[...], views[:, t * CH : (t + 1) * CH]).T
    other = 1 - my_c
    twin = (z, at(my_x * CN + other, my_y))

    def half_of(ref, c):
        return ref.at[pl.ds(pl.multiple_of(c * half, 16), half)]

    send(half_of(csend, other), crecv, sems.at[6], sems.at[7], twin)
    wait_for(crecv, sems.at[7])
    total = half_of(csend, my_c)[...] + crecv[...]
    padding = jnp.zeros((zn, -share % 16, CH), F32)
    parts = jnp.concatenate([total.reshape(zn, share, CH), padding], axis=1)
    zsend[...] = parts.astype(BF)
    if zn > 1:
        repeat(1, zn, lambda k: send(
            zsend.at[z_peer(k)], zrecv.at[z], sems.at[8], sems.at[9], (z_peer(k), me)))
    zrecv[z] = zsend[z]
    step_exchange(1, xc_n, *second)
    if zn > 1:
        wait_for(zrecv.at[pl.ds(0, zn - 1)], sems.at[9])
    total = zrecv[0].astype(F32)
    for k in range(1, zn):
        total = total + zrecv[k].astype(F32)
    xgot[my_x] = total
    if XN > 1:
        repeat(1, XN, lambda k: send(
            xgot.at[my_x], xgot.at[my_x], sems.at[10], sems.at[11],
            (z, at(lax.rem(my_x + k, XN) * CN + my_c, my_y))))
    step_exchange(2, xc_n, *second)
    if XN > 1:
        wait_for(xgot.at[pl.ds(0, XN - 1)], sems.at[11])
    total = xgot[0]
    for k in range(1, XN):
        total = total + xgot[k]
    ygot[my_y] = total.astype(BF)
    repeat(1, YN, lambda k: send(
        ygot.at[my_y], ygot.at[my_y], sems.at[12], sems.at[13], (z, at(my_xc, wrap_y(k)))))
    step_exchange(3, xc_n, *second)
    wait_for(ygot.at[pl.ds(0, YN - 1)], sems.at[13])
    total = ygot[0].astype(F32)
    for k in range(1, YN):
        total = total + ygot[k].astype(F32)
    zgath[z] = total.astype(BF)
    if zn > 1:
        repeat(1, zn, lambda k: send(zgath.at[z], zgath.at[z], sems.at[14], sems.at[15], (z_peer(k), me)))

    wait_for(flat(got_b), sems_b.at[1])
    run[0] = jnp.zeros((64, CH), F32)

    def add_up(xc):
        for s in range(8):
            j = xc * 8 + s
            run[j + 1] = run[prev[j]] + got_b[xc, s].astype(F32)

    repeat(0, xc_n, add_up)
    for f in range(FACES):
        ghost[f] = run[last[f]]
    if zn > 1:
        wait_for(zgath.at[pl.ds(0, zn - 1)], sems.at[15])
    send(zgath, cgath, sems.at[16], sems.at[17], twin)
    build_views(cube, ghost, shifted, views)
    for b in range(2 * NB):
        rows = slice(b * VOX // 2, (b + 1) * VOX // 2)
        grad = product(views[rows, :], wback[...])
        grad_out[rows, :] = (mask[rows, :] * grad).astype(BF)

    wait_for(cgath, sems.at[17])
    half_of(wg_out, my_c)[...] = zgath[:, :share].astype(F32).reshape(half, CH) * scale
    half_of(wg_out, other)[...] = cgath[:, :share].astype(F32).reshape(half, CH) * scale

    drain(rows_a, up_a, down_a, chain_a, sems_a)
    drain(rows_b, up_b, down_b, chain_b, sems_b)
    wait_for(meta_out.at[pl.ds(0, 6)], sems.at[4])
    wait_for(crecv, sems.at[6])
    if zn > 1:
        wait_for(zsend.at[pl.ds(0, zn - 1)], sems.at[8])
        wait_for(zgath.at[pl.ds(0, zn - 1)], sems.at[14])
    if XN > 1:
        wait_for(xgot.at[pl.ds(0, XN - 1)], sems.at[10])
    wait_for(ygot.at[pl.ds(0, YN - 1)], sems.at[12])
    wait_for(zgath, sems.at[16])


def on_device(zn, gn, features, occupancy, weights, cotangent, send_count, send_face, recv_face):
    vmem = pl.BlockSpec(memory_space=pltpu.VMEM)
    anywhere = pl.BlockSpec(memory_space=pl.ANY)
    xc_n = XN * CN
    half = TAPS * CH // CN
    share = half // zn
    padded = -(-share // 16) * 16
    scale = float(zn * gn * ROWS) ** (-0.5)
    shells = [pltpu.VMEM((FACES, 64, CH), BF) for _ in range(3)]
    activated, grad, weight_grad = pl.pallas_call(
        functools.partial(kernel, zn, gn, scale),
        out_shape=(
            jax.ShapeDtypeStruct((ROWS, CH), BF),
            jax.ShapeDtypeStruct((ROWS, CH), BF),
            jax.ShapeDtypeStruct((TAPS * CH, CH), F32),
        ),
        in_specs=[anywhere] * 7,
        out_specs=(vmem, vmem, vmem),
        scratch_shapes=[
            pltpu.VMEM((ROWS, CH), BF),
            pltpu.VMEM((NB, VOX), jnp.int32),
            pltpu.VMEM((TAPS * CH, CH), BF),
            pltpu.VMEM((ROWS, CH), BF),
            pltpu.SMEM((gn,), jnp.int32),
            pltpu.SMEM((gn,), jnp.int32),
            pltpu.SMEM((gn,), jnp.int32),
            pltpu.VMEM((ROWS, CH), F32),
            pltpu.VMEM((ROWS, CH), F32),
            pltpu.VMEM((FACES, 64, CH), F32),
            pltpu.VMEM((VOX, CH), F32),
            pltpu.VMEM((ROWS, TAPS * CH), BF),
            pltpu.VMEM((TAPS * CH, CH), BF),
            pltpu.VMEM((CH, ROWS), BF),
            pltpu.VMEM((gn + 1, 64, CH), F32),
            pltpu.SMEM((gn,), jnp.int32),
            pltpu.SMEM((gn,), jnp.int32),
            pltpu.SMEM((gn,), jnp.int32),
            pltpu.SMEM((YN, 2 * xc_n), jnp.int32),
            pltpu.SMEM((YN, 2 * xc_n), jnp.int32),
            pltpu.VMEM((FACES, 64, CH), BF),
            pltpu.VMEM((FACES, 64, CH), BF),
            pltpu.VMEM((xc_n, 8, 64, CH), BF),
            pltpu.VMEM((xc_n, 8, 64, CH), BF),
            pltpu.VMEM((xc_n, 8, 64, CH), BF),
            pltpu.VMEM((xc_n, 8, 64, CH), BF),
            shells, shells, shells, shells,
            pltpu.VMEM((TAPS * CH, CH), F32),
            pltpu.VMEM((half, CH), F32),
            pltpu.VMEM((zn, padded, CH), BF),
            pltpu.VMEM((zn, padded, CH), BF),
            pltpu.VMEM((XN, padded, CH), F32),
            pltpu.VMEM((YN, padded, CH), BF),
            pltpu.VMEM((zn, padded, CH), BF),
            pltpu.VMEM((zn, padded, CH), BF),
            pltpu.SemaphoreType.DMA((7,)),
            pltpu.SemaphoreType.DMA((24,)),
            pltpu.SemaphoreType.DMA((24,)),
            pltpu.SemaphoreType.DMA((18,)),
        ],
        compiler_params=pltpu.CompilerParams(
            collective_id=0, has_side_effects=True, vmem_limit_bytes=40 * 1024 * 1024
        ),
        cost_estimate=pl.CostEstimate(
            flops=6 * ROWS * TAPS * CH * CH, bytes_accessed=2000000, transcendentals=ROWS * CH
        ),
    )(
        features.reshape(ROWS, CH),
        occupancy,
        weights.reshape(TAPS * CH, CH),
        cotangent.reshape(ROWS, CH),
        send_count.reshape(gn),
        send_face.reshape(gn),
        recv_face.reshape(gn),
    )
    return (
        activated.reshape(NB, VOX, CH),
        grad.reshape(NB, VOX, CH),
        weight_grad.reshape(TAPS, CH, CH),
    )


def solution(mesh):
    zn, gn = mesh.shape["gx"], mesh.shape["gy"]
    split = P(("gx", "gy"), None, None)
    return jax.shard_map(
        functools.partial(on_device, zn, gn),
        mesh=mesh,
        in_specs=(split, P(("gx", "gy"), None), P(), split, P(("gx", "gy"), None), split, split),
        out_specs=(split, split, P()),
        check_vma=False,
    )
```

time: 91.9 us -> 80.5 us (0.88)
  Pallas kernels: 85.3 us -> 73.9 us
    pallas_call x1, Pallas kernels: 85.3 us -> 73.9 us  [on_device(): pl.pallas_call(functools.partial(kernel, zn, gn, scale), out_shape=(jax.S...]
where the time goes in v2:
time: 80.5 us; the launch traced here: 80.3 us
  Pallas kernels  73.9 us (92%)
  local copies, waits for them, and re-layouts  5.68 us (7%)
    pallas_call x1, Pallas kernels, on_device(): pl.pallas_call(functools.partial(kernel, zn, gn, scale), out_shape=(jax.S...  73.9 us
    unnamed x17, local copies, waits for them, and re-layouts  5.68 us

profile of v2, /device:TPU:1, one launch (start us, length us, event | category | flops | bytes accessed | tf_op | source)
XLA Modules:
  0.0 80.3 jit_solution(16714579207165343118)
XLA Ops:
  0.6 0.0 copy-start.3
  0.6 0.0 copy-start.4
  0.7 0.0 copy-start.5
  0.7 0.0 copy-start.6
  0.7 0.6 copy-done.3
  1.3 0.0 copy-done.4
  1.3 0.0 copy-done.5
  1.3 0.0 copy-done.6
  1.3 0.0 copy-start
  1.3 0.9 %copy-done = bf16[2,512,128]{2,1,0:T(8,128)(2,1)S(1)} copy-done((bf16[2,512,128]{2,1,0:T(8,128)(2,1)S(1)}, bf16[2,512,128]{2,1,0:T(8,128)(2,1)}, u32[]{:S(2)}) %copy-start) | copy-done | bytes 262168
  2.3 0.0 copy-start.1
  2.3 0.9 %copy-done.1 = bf16[2,512,128]{2,1,0:T(8,128)(2,1)S(1)} copy-done((bf16[2,512,128]{2,1,0:T(8,128)(2,1)S(1)}, bf16[2,512,128]{2,1,0:T(8,128)(2,1)}, u32[]{:S(2)}) %copy-start.1) | copy-done | bytes 262168
  3.2 0.0 copy-start.2
  3.2 0.9 %copy-done.2 = bf16[7,128,128]{2,1,0:T(8,128)(2,1)S(1)} copy-done((bf16[7,128,128]{2,1,0:T(8,128)(2,1)S(1)}, bf16[7,128,128]{2,1,0:T(8,128)(2,1)}, u32[]{:S(2)}) %copy-start.2) | copy-done | bytes 229400
  4.2 73.9 %shard_map.94 = (bf16[1024,128]{1,0:T(8,128)(2,1)S(1)}, bf16[1024,128]{1,0:T(8,128)(2,1)S(1)}, f32[896,128]{1,0:T(8,128)S(1)}) custom-call(bf16[1024,128]{1,0:T(8,128)(2,1)S(1)} %bitcast.12, s32[2,512]{1,0:T(2,128)S(1)} %copy-done.3, bf16[896,128]{1,0:T(8,128)(2,1)S(1)} %bitcast.14, bf16[1024,128]{1,0:T(8,128)(2,1)S(1)} %bitcast.13, s32[64]{0:T(128)S(1)} %bitcast.15, ...), custom_call_target="tpu_custom_call" | custom-call | flops 704643072 | bytes 2000000 | tf_op jit(solution)/shard_map/pallas_call | solution.py:380
  78.1 0.7 copy.13
  78.8 0.7 copy.14
  79.5 0.8 copy.15
Async XLA Ops:
  0.6 0.7 copy-start.3
  0.6 0.7 copy-start.4
  0.7 0.7 copy-start.5
  0.7 0.7 copy-start.6
  1.3 0.9 %copy-start = (bf16[2,512,128]{2,1,0:T(8,128)(2,1)S(1)}, bf16[2,512,128]{2,1,0:T(8,128)(2,1)}, u32[]{:S(2)}) copy-start(bf16[2,512,128]{2,1,0:T(8,128)(2,1)} %param.7) | copy-start | bytes 786436
  2.3 0.9 %copy-start.1 = (bf16[2,512,128]{2,1,0:T(8,128)(2,1)S(1)}, bf16[2,512,128]{2,1,0:T(8,128)(2,1)}, u32[]{:S(2)}) copy-start(bf16[2,512,128]{2,1,0:T(8,128)(2,1)} %param.10) | copy-start | bytes 786436
  3.2 0.9 %copy-start.2 = (bf16[7,128,128]{2,1,0:T(8,128)(2,1)S(1)}, bf16[7,128,128]{2,1,0:T(8,128)(2,1)}, u32[]{:S(2)}) copy-start(bf16[7,128,128]{2,1,0:T(8,128)(2,1)} %param.9) | copy-start | bytes 688132

commit v3 on v2

--- a/solution.py
+++ b/solution.py
@@ -71,7 +71,7 @@
     feat_in, occ_in, wcat_in, cot_in, count_in, sface_in, rface_in,
     act_out, grad_out, wg_out,
     feat, occ, wcat, cot, count, sface, rface,
-    mask, cube, ghost, shifted, views, wback, delta_t, run, prev, slot_face, slot_row, meta_out, meta_in,
+    mask, cube, ghost, shifted, views, wback, delta_t, run, prev, slot_face, slot_row, meta_out, meta_in, meta_far,
     faces_a, faces_b, rows_a, rows_b, got_a, got_b, up_a, down_a, up_b, down_b,
     csend, crecv, zsend, zrecv, xgot, ygot, zgath, cgath,
     load_sems, chain_a, chain_b, sems,
@@ -121,7 +121,8 @@
 
     repeat(1, YN, lambda k: greet((z, at(my_xc, wrap_y(k)))))
     repeat(1, xc_n, lambda k: greet((z, at(xc_peer(k), my_y))))
-    repeat(1, xc_n, lambda k: greet((z, at(xc_peer(k), wrap_y(4)))))
+    repeat(1, xc_n, lambda k: greet((z, at(xc_peer(k), wrap_y(1)))))
+    repeat(1, xc_n, lambda k: greet((z, at(xc_peer(k), wrap_y(-1)))))
     if zn > 1:
         repeat(1, zn, lambda k: greet((z_peer(k), me)))
 
@@ -164,19 +165,11 @@
             part = pl.ds(p * 4, 4)
             send(faces.at[part], up[0].at[part], chain.at[0], chain.at[6 + p], (z, at(my_xc, wrap_y(1))))
             send(faces.at[part], down[0].at[part], chain.at[3], chain.at[6 + 9 + p], (z, at(my_xc, wrap_y(-1))))
-        far = wrap_y(4)
 
         def pick(xc):
             rows[xc, 0] = faces[meta_out[my_y, column + xc]]
-            rows[xc, 1] = faces[meta_out[far, column + xc]]
 
         repeat(0, xc_n, pick)
-
-        def ship(k):
-            xc = xc_peer(k)
-            send(rows.at[xc, 1], got.at[my_xc, 1], row_sems.at[0], row_sems.at[1], (z, at(xc, far)))
-
-        repeat(0, xc_n, ship)
 
         def ship_own(k):
             xc = xc_peer(k)
@@ -204,6 +197,17 @@
 
         repeat(0, xc_n, pick)
         pair = pl.ds(2 * d, 2)
+        if d == 3:
+            def pick_up(xc):
+                rows[xc, 1] = up[2][meta_far[low, column + xc]]
+                send(rows.at[xc, 1], got.at[my_xc, 1], row_sems.at[0], row_sems.at[1], (z, at(xc, wrap_y(1))))
+
+            def pick_down(xc):
+                rows[xc, 1] = down[2][meta_far[high, column + xc]]
+                send(rows.at[xc, 1], got.at[my_xc, 1], row_sems.at[0], row_sems.at[1], (z, at(xc, wrap_y(-1))))
+
+            repeat(0, xc_n // 2, pick_up)
+            repeat(xc_n // 2, xc_n, pick_down)
 
         def ship(k):
             xc = xc_peer(k)
@@ -223,11 +227,13 @@
             wait_for(down[d], chain.at[3 + d])
         wait_for(flat(rows), row_sems.at[0])
 
-    pl.semaphore_wait(barrier, (YN - 1) + 2 * (xc_n - 1) + (zn - 1))
+    pl.semaphore_wait(barrier, (YN - 1) + 3 * (xc_n - 1) + (zn - 1))
     sems_a, sems_b = sems.at[pl.ds(0, 2)], sems.at[pl.ds(2, 2)]
     for d in (1, -1, 2, -2, 3, -3):
         y = wrap_y(d)
         send(meta_out.at[y], meta_in.at[my_y], sems.at[4], sems.at[5], (z, at(my_xc, y)))
+    for d in (3, -3):
+        send(meta_out.at[wrap_y(4)], meta_far.at[my_y], sems.at[18], sems.at[19], (z, at(my_xc, wrap_y(d))))
     first = (rows_a, got_a, up_a, down_a, chain_a, sems_a)
     second = (rows_b, got_b, up_b, down_b, chain_b, sems_b)
     start_exchange(faces_a, 0, *first)
@@ -263,6 +269,7 @@
         return tuple(jnp.where(face == f, j + 1, last[f]) for f in range(FACES))
 
     last = lax.fori_loop(0, gn, chain_up, tuple(jnp.int32(0) for _ in range(FACES)))
+    wait_for(meta_far.at[pl.ds(0, 2)], sems.at[19])
     step_exchange(3, 0, *first)
 
     wait_for(flat(got_a), sems_a.at[1])
@@ -303,6 +310,7 @@
             zsend.at[z_peer(k)], zrecv.at[z], sems.at[8], sems.at[9], (z_peer(k), me)))
     zrecv[z] = zsend[z]
     step_exchange(1, xc_n, *second)
+    step_exchange(2, xc_n, *second)
     if zn > 1:
         wait_for(zrecv.at[pl.ds(0, zn - 1)], sems.at[9])
     total = zrecv[0].astype(F32)
@@ -313,7 +321,6 @@
         repeat(1, XN, lambda k: send(
             xgot.at[my_x], xgot.at[my_x], sems.at[10], sems.at[11],
             (z, at(lax.rem(my_x + k, XN) * CN + my_c, my_y))))
-    step_exchange(2, xc_n, *second)
     if XN > 1:
         wait_for(xgot.at[pl.ds(0, XN - 1)], sems.at[11])
     total = xgot[0]
@@ -358,6 +365,7 @@
     drain(rows_a, up_a, down_a, chain_a, sems_a)
     drain(rows_b, up_b, down_b, chain_b, sems_b)
     wait_for(meta_out.at[pl.ds(0, 6)], sems.at[4])
+    wait_for(meta_out.at[pl.ds(0, 2)], sems.at[18])
     wait_for(crecv, sems.at[6])
     if zn > 1:
         wait_for(zsend.at[pl.ds(0, zn - 1)], sems.at[8])
@@ -370,7 +378,7 @@
 
 def on_device(zn, gn, features, occupancy, weights, cotangent, send_count, send_face, recv_face):
     vmem = pl.BlockSpec(memory_space=pltpu.VMEM)
-    anywhere = pl.BlockSpec(memory_space=pl.ANY)
+    anywhere = pl.BlockSpec(memory_space=pltpu.HBM)
     xc_n = XN * CN
     half = TAPS * CH // CN
     share = half // zn
@@ -407,6 +415,7 @@
             pltpu.SMEM((gn,), jnp.int32),
             pltpu.SMEM((YN, 2 * xc_n), jnp.int32),
             pltpu.SMEM((YN, 2 * xc_n), jnp.int32),
+            pltpu.SMEM((YN, 2 * xc_n), jnp.int32),
             pltpu.VMEM((FACES, 64, CH), BF),
             pltpu.VMEM((FACES, 64, CH), BF),
             pltpu.VMEM((xc_n, 8, 64, CH), BF),
@@ -425,10 +434,10 @@
             pltpu.SemaphoreType.DMA((7,)),
             pltpu.SemaphoreType.DMA((24,)),
             pltpu.SemaphoreType.DMA((24,)),
-            pltpu.SemaphoreType.DMA((18,)),
+            pltpu.SemaphoreType.DMA((20,)),
         ],
         compiler_params=pltpu.CompilerParams(
-            collective_id=0, has_side_effects=True, vmem_limit_bytes=40 * 1024 * 1024
+            collective_id=0, has_side_effects=True, vmem_limit_bytes=62 * 1024 * 1024
         ),
         cost_estimate=pl.CostEstimate(
             flops=6 * ROWS * TAPS * CH * CH, bytes_accessed=2000000, transcendentals=ROWS * CH

time: 80.5 us -> 73 us (0.907)
  Pallas kernels: 73.9 us -> 69 us
  local copies, waits for them, and re-layouts: 5.68 us -> 3.22 us
    pallas_call x1, Pallas kernels: 73.9 us -> 69 us  [on_device(): pl.pallas_call(functools.partial(kernel, zn, gn, scale), out_shape=(jax.S...]
    unnamed x17 -> x7, local copies, waits for them, and re-layouts: 5.68 us -> 3.22 us
where the time goes in v3:
time: 73 us; the launch traced here: 72.9 us
  Pallas kernels  69 us (95%)
  local copies, waits for them, and re-layouts  3.22 us (4%)
    pallas_call x1, Pallas kernels, on_device(): pl.pallas_call(functools.partial(kernel, zn, gn, scale), out_shape=(jax.S...  69 us
    unnamed x7, local copies, waits for them, and re-layouts  3.22 us

profile of v3, /device:TPU:1, one launch (start us, length us, event | category | flops | bytes accessed | tf_op | source)
XLA Modules:
  0.0 72.9 jit_solution(6792216112676539669)
XLA Ops:
  0.6 69.0 %shard_map.94 = (bf16[1024,128]{1,0:T(8,128)(2,1)}, bf16[1024,128]{1,0:T(8,128)(2,1)}, f32[896,128]{1,0:T(8,128)}) custom-call(bf16[1024,128]{1,0:T(8,128)(2,1)} %bitcast.12, s32[2,512]{1,0:T(2,128)} %occ_in.1, bf16[896,128]{1,0:T(8,128)(2,1)} %bitcast.14, bf16[1024,128]{1,0:T(8,128)(2,1)} %bitcast.13, s32[64]{0:T(128)} %bitcast.15, s32[64]{0:T(128)} %bitcast.16, ...), custom_call_target="tpu_custom_call" | custom-call | flops 704643072 | bytes 2000000 | tf_op jit(solution)/shard_map/pallas_call | solution.py:388
  69.6 0.0 copy-start.1
  69.6 0.0 copy-start
  69.7 1.7 %copy.13 = bf16[2,512,128]{2,1,0:T(8,128)(2,1)} copy(bf16[2,512,128]{2,1,0:T(8,128)(2,1)} %bitcast.11) | data formatting | bytes 524288
  71.4 0.0 copy-done.1
  71.4 0.7 copy.14
  72.1 0.0 copy-done
  72.1 0.8 %copy.15 = f32[7,128,128]{2,1,0:T(8,128)} copy(f32[7,128,128]{2,1,0:T(8,128)S(1)} %bitcast.9) | data formatting | bytes 917504
Async XLA Ops:
  69.6 1.8 %copy-start.1 = (bf16[1024,128]{1,0:T(8,128)(2,1)S(1)}, bf16[1024,128]{1,0:T(8,128)(2,1)}, u32[]{:S(2)}) copy-start(bf16[1024,128]{1,0:T(8,128)(2,1)} %get-tuple-element.7) | copy-start | bytes 786436
  69.6 2.5 %copy-start = (f32[896,128]{1,0:T(8,128)S(1)}, f32[896,128]{1,0:T(8,128)}, u32[]{:S(2)}) copy-start(f32[896,128]{1,0:T(8,128)} %get-tuple-element.8) | copy-start | bytes 1376260

commit v4 on v3

--- a/solution.py
+++ b/solution.py
@@ -67,14 +67,14 @@
 
 
 def kernel(
-    zn, gn, scale,
+    zn, gn,
     feat_in, occ_in, wcat_in, cot_in, count_in, sface_in, rface_in,
     act_out, grad_out, wg_out,
     feat, occ, wcat, cot, count, sface, rface,
     mask, cube, ghost, shifted, views, wback, delta_t, run, prev, slot_face, slot_row, meta_out, meta_in, meta_far,
     faces_a, faces_b, rows_a, rows_b, got_a, got_b, up_a, down_a, up_b, down_b,
-    csend, crecv, zsend, zrecv, xgot, ygot, zgath, cgath,
-    load_sems, chain_a, chain_b, sems,
+    csend, crecv, zsend, zrecv, ygot, zgath, cgath, act, grad,
+    load_sems, out_sems, chain_a, chain_b, sems,
 ):
     z = lax.axis_index("gx")
     me = lax.axis_index("gy")
@@ -84,7 +84,9 @@
     my_c = lax.rem(me, CN)
     my_xc = my_x * CN + my_c
     half = TAPS * CH // CN
-    share = half // zn
+    en = zn * XN
+    me_e = z * XN + my_x
+    piece = zrecv.shape[1]
 
     def wrap_y(offset):
         return lax.rem(my_y + offset + YN, YN)
@@ -95,8 +97,11 @@
     def xc_peer(k):
         return lax.rem(my_xc + k, xc_n)
 
-    def z_peer(k):
-        return lax.rem(z + k, zn)
+    def zx_peer(k):
+        return lax.rem(me_e + k, en)
+
+    def zx_device(e):
+        return (e // XN, at(lax.rem(e, XN) * CN + my_c, my_y))
 
     def repeat(low, high, body):
         def step(i, _):
@@ -123,8 +128,7 @@
     repeat(1, xc_n, lambda k: greet((z, at(xc_peer(k), my_y))))
     repeat(1, xc_n, lambda k: greet((z, at(xc_peer(k), wrap_y(1)))))
     repeat(1, xc_n, lambda k: greet((z, at(xc_peer(k), wrap_y(-1)))))
-    if zn > 1:
-        repeat(1, zn, lambda k: greet((z_peer(k), me)))
+    repeat(XN, en, lambda k: greet(zx_device(lax.rem(z * XN + k, en))))
 
     loads = [
         pltpu.make_async_copy(src, dst, load_sems.at[i])
@@ -227,7 +231,7 @@
             wait_for(down[d], chain.at[3 + d])
         wait_for(flat(rows), row_sems.at[0])
 
-    pl.semaphore_wait(barrier, (YN - 1) + 3 * (xc_n - 1) + (zn - 1))
+    pl.semaphore_wait(barrier, (YN - 1) + 3 * (xc_n - 1) + (zn - 1) * XN)
     sems_a, sems_b = sems.at[pl.ds(0, 2)], sems.at[pl.ds(2, 2)]
     for d in (1, -1, 2, -2, 3, -3):
         y = wrap_y(d)
@@ -238,6 +242,13 @@
     second = (rows_b, got_b, up_b, down_b, chain_b, sems_b)
     start_exchange(faces_a, 0, *first)
 
+    wait_for(meta_in.at[pl.ds(0, 6)], sems.at[5])
+    step_exchange(1, 0, *first)
+    step_exchange(2, 0, *first)
+
+    wait_for(meta_far.at[pl.ds(0, 2)], sems.at[19])
+    step_exchange(3, 0, *first)
+
     def list_slots(xc):
         for s in range(8):
             p = at(xc, wrap_y(ROW_OF[s]))
@@ -251,15 +262,6 @@
         return tuple(jnp.where(row == f, j, found[f]) for f in range(FACES))
 
     source = lax.fori_loop(0, gn, find_source, tuple(jnp.int32(-1) for _ in range(FACES)))
-    loads[5].wait()
-    loads[6].wait()
-    wait_for(meta_in.at[pl.ds(0, 6)], sems.at[5])
-    step_exchange(1, 0, *first)
-    for t in range(TAPS):
-        o = OPPOSITE[t]
-        wback[t * CH : (t + 1) * CH, :] = wcat[o * CH : (o + 1) * CH, :].astype(F32).T.astype(BF)
-    step_exchange(2, 0, *first)
-
     def chain_up(j, last):
         face = slot_face[j]
         before = jnp.int32(0)
@@ -269,8 +271,11 @@
         return tuple(jnp.where(face == f, j + 1, last[f]) for f in range(FACES))
 
     last = lax.fori_loop(0, gn, chain_up, tuple(jnp.int32(0) for _ in range(FACES)))
-    wait_for(meta_far.at[pl.ds(0, 2)], sems.at[19])
-    step_exchange(3, 0, *first)
+    loads[5].wait()
+    loads[6].wait()
+    for t in range(TAPS):
+        o = OPPOSITE[t]
+        wback[t * CH : (t + 1) * CH, :] = wcat[o * CH : (o + 1) * CH, :].astype(F32).T.astype(BF)
 
     wait_for(flat(got_a), sems_a.at[1])
     for f in range(FACES):
@@ -284,11 +289,13 @@
         preact = product(views[rows, :], wcat[...])
         sigma = jax.nn.sigmoid(preact)
         flags = mask[rows, :]
-        act_out[rows, :] = (flags * preact * sigma).astype(BF)
+        act[rows, :] = (flags * preact * sigma).astype(BF)
         delta = (cot[rows, :].astype(F32) * flags * sigma * (1.0 + preact * (1.0 - sigma))).astype(BF)
         cube[rows, :] = delta.astype(F32)
     cut_faces(cube, faces_b)
     start_exchange(faces_b, xc_n, *second)
+    store_act = pltpu.make_async_copy(act, act_out, out_sems.at[0])
+    store_act.start()
 
     delta_t[...] = cube[...].T.astype(BF)
     for t in range(TAPS):
@@ -302,41 +309,33 @@
     send(half_of(csend, other), crecv, sems.at[6], sems.at[7], twin)
     wait_for(crecv, sems.at[7])
     total = half_of(csend, my_c)[...] + crecv[...]
-    padding = jnp.zeros((zn, -share % 16, CH), F32)
-    parts = jnp.concatenate([total.reshape(zn, share, CH), padding], axis=1)
-    zsend[...] = parts.astype(BF)
-    if zn > 1:
-        repeat(1, zn, lambda k: send(
-            zsend.at[z_peer(k)], zrecv.at[z], sems.at[8], sems.at[9], (z_peer(k), me)))
-    zrecv[z] = zsend[z]
+    zsend[0:half, :] = total.astype(BF)
+    if en * piece > half:
+        zsend[half:, :] = jnp.zeros((en * piece - half, CH), BF)
+
+    def piece_of(ref, e):
+        return ref.at[pl.ds(pl.multiple_of(e * piece, 16), piece)]
+
+    def scatter(k):
+        e = zx_peer(k)
+        send(piece_of(zsend, e), zrecv.at[me_e], sems.at[8], sems.at[9], zx_device(e))
+
+    repeat(1, en, scatter)
+    zrecv[me_e] = piece_of(zsend, me_e)[...]
     step_exchange(1, xc_n, *second)
     step_exchange(2, xc_n, *second)
-    if zn > 1:
-        wait_for(zrecv.at[pl.ds(0, zn - 1)], sems.at[9])
-    total = zrecv[0].astype(F32)
-    for k in range(1, zn):
-        total = total + zrecv[k].astype(F32)
-    xgot[my_x] = total
-    if XN > 1:
-        repeat(1, XN, lambda k: send(
-            xgot.at[my_x], xgot.at[my_x], sems.at[10], sems.at[11],
-            (z, at(lax.rem(my_x + k, XN) * CN + my_c, my_y))))
-    if XN > 1:
-        wait_for(xgot.at[pl.ds(0, XN - 1)], sems.at[11])
-    total = xgot[0]
-    for k in range(1, XN):
-        total = total + xgot[k]
-    ygot[my_y] = total.astype(BF)
+    wait_for(zrecv.at[pl.ds(0, en - 1)], sems.at[9])
+    ygot[my_y] = jnp.sum(zrecv[...].astype(F32), axis=0)
     repeat(1, YN, lambda k: send(
         ygot.at[my_y], ygot.at[my_y], sems.at[12], sems.at[13], (z, at(my_xc, wrap_y(k)))))
     step_exchange(3, xc_n, *second)
     wait_for(ygot.at[pl.ds(0, YN - 1)], sems.at[13])
-    total = ygot[0].astype(F32)
+    total = ygot[0]
     for k in range(1, YN):
-        total = total + ygot[k].astype(F32)
-    zgath[z] = total.astype(BF)
-    if zn > 1:
-        repeat(1, zn, lambda k: send(zgath.at[z], zgath.at[z], sems.at[14], sems.at[15], (z_peer(k), me)))
+        total = total + ygot[k]
+    mine = piece_of(zgath, me_e)
+    mine[...] = total.astype(BF)
+    repeat(1, en, lambda k: send(mine, mine, sems.at[14], sems.at[15], zx_device(zx_peer(k))))
 
     wait_for(flat(got_b), sems_b.at[1])
     run[0] = jnp.zeros((64, CH), F32)
@@ -349,31 +348,40 @@
     repeat(0, xc_n, add_up)
     for f in range(FACES):
         ghost[f] = run[last[f]]
-    if zn > 1:
-        wait_for(zgath.at[pl.ds(0, zn - 1)], sems.at[15])
-    send(zgath, cgath, sems.at[16], sems.at[17], twin)
+    wait_for(zgath.at[pl.ds(0, (en - 1) * piece)], sems.at[15])
+    send(zgath.at[pl.ds(0, half)], cgath, sems.at[16], sems.at[17], twin)
     build_views(cube, ghost, shifted, views)
     for b in range(2 * NB):
         rows = slice(b * VOX // 2, (b + 1) * VOX // 2)
-        grad = product(views[rows, :], wback[...])
-        grad_out[rows, :] = (mask[rows, :] * grad).astype(BF)
-
+        grad[rows, :] = (mask[rows, :] * product(views[rows, :], wback[...])).astype(BF)
+
+    store_grad = pltpu.make_async_copy(grad, grad_out, out_sems.at[1])
+    store_grad.start()
+    store_own = pltpu.make_async_copy(zgath.at[pl.ds(0, half)], half_of(wg_out, my_c), out_sems.at[2])
+    store_own.start()
     wait_for(cgath, sems.at[17])
-    half_of(wg_out, my_c)[...] = zgath[:, :share].astype(F32).reshape(half, CH) * scale
-    half_of(wg_out, other)[...] = cgath[:, :share].astype(F32).reshape(half, CH) * scale
+    store_other = pltpu.make_async_copy(cgath, half_of(wg_out, other), out_sems.at[3])
+    store_other.start()
 
     drain(rows_a, up_a, down_a, chain_a, sems_a)
     drain(rows_b, up_b, down_b, chain_b, sems_b)
     wait_for(meta_out.at[pl.ds(0, 6)], sems.at[4])
     wait_for(meta_out.at[pl.ds(0, 2)], sems.at[18])
     wait_for(crecv, sems.at[6])
-    if zn > 1:
-        wait_for(zsend.at[pl.ds(0, zn - 1)], sems.at[8])
-        wait_for(zgath.at[pl.ds(0, zn - 1)], sems.at[14])
-    if XN > 1:
-        wait_for(xgot.at[pl.ds(0, XN - 1)], sems.at[10])
+    wait_for(zsend.at[pl.ds(0, (en - 1) * piece)], sems.at[8])
     wait_for(ygot.at[pl.ds(0, YN - 1)], sems.at[12])
-    wait_for(zgath, sems.at[16])
+    wait_for(zgath.at[pl.ds(0, (en - 1) * piece)], sems.at[14])
+    wait_for(cgath, sems.at[16])
+    store_act.wait()
+    store_grad.wait()
+    store_own.wait()
+    store_other.wait()
+
+
+def finish(scale, act_in, grad_in, wg_in, act_out, grad_out, wg_out):
+    act_out[...] = act_in[...]
+    grad_out[...] = grad_in[...]
+    wg_out[...] = wg_in[...].astype(F32) * scale
 
 
 def on_device(zn, gn, features, occupancy, weights, cotangent, send_count, send_face, recv_face):
@@ -381,19 +389,19 @@
     anywhere = pl.BlockSpec(memory_space=pltpu.HBM)
     xc_n = XN * CN
     half = TAPS * CH // CN
-    share = half // zn
-    padded = -(-share // 16) * 16
+    en = zn * XN
+    piece = -(-half // (16 * en)) * 16
     scale = float(zn * gn * ROWS) ** (-0.5)
     shells = [pltpu.VMEM((FACES, 64, CH), BF) for _ in range(3)]
     activated, grad, weight_grad = pl.pallas_call(
-        functools.partial(kernel, zn, gn, scale),
+        functools.partial(kernel, zn, gn),
         out_shape=(
             jax.ShapeDtypeStruct((ROWS, CH), BF),
             jax.ShapeDtypeStruct((ROWS, CH), BF),
-            jax.ShapeDtypeStruct((TAPS * CH, CH), F32),
+            jax.ShapeDtypeStruct((TAPS * CH, CH), BF),
         ),
         in_specs=[anywhere] * 7,
-        out_specs=(vmem, vmem, vmem),
+        out_specs=(anywhere, anywhere, anywhere),
         scratch_shapes=[
             pltpu.VMEM((ROWS, CH), BF),
             pltpu.VMEM((NB, VOX), jnp.int32),
@@ -425,13 +433,15 @@
             shells, shells, shells, shells,
             pltpu.VMEM((TAPS * CH, CH), F32),
             pltpu.VMEM((half, CH), F32),
-            pltpu.VMEM((zn, padded, CH), BF),
-            pltpu.VMEM((zn, padded, CH), BF),
-            pltpu.VMEM((XN, padded, CH), F32),
-            pltpu.VMEM((YN, padded, CH), BF),
-            pltpu.VMEM((zn, padded, CH), BF),
-            pltpu.VMEM((zn, padded, CH), BF),
+            pltpu.VMEM((en * piece, CH), BF),
+            pltpu.VMEM((en, piece, CH), BF),
+            pltpu.VMEM((YN, piece, CH), F32),
+            pltpu.VMEM((en * piece, CH), BF),
+            pltpu.VMEM((half, CH), BF),
+            pltpu.VMEM((ROWS, CH), BF),
+            pltpu.VMEM((ROWS, CH), BF),
             pltpu.SemaphoreType.DMA((7,)),
+            pltpu.SemaphoreType.DMA((4,)),
             pltpu.SemaphoreType.DMA((24,)),
             pltpu.SemaphoreType.DMA((24,)),
             pltpu.SemaphoreType.DMA((20,)),
@@ -451,6 +461,17 @@
         send_face.reshape(gn),
         recv_face.reshape(gn),
     )
+    activated, grad, weight_grad = pl.pallas_call(
+        functools.partial(finish, scale),
+        out_shape=(
+            jax.ShapeDtypeStruct((ROWS, CH), BF),
+            jax.ShapeDtypeStruct((ROWS, CH), BF),
+            jax.ShapeDtypeStruct((TAPS * CH, CH), F32),
+        ),
+        in_specs=[vmem, vmem, vmem],
+        out_specs=(vmem, vmem, vmem),
+        compiler_params=pltpu.CompilerParams(vmem_limit_bytes=62 * 1024 * 1024),
+    )(activated, grad, weight_grad)
     return (
         activated.reshape(NB, VOX, CH),
         grad.reshape(NB, VOX, CH),

time: 73 us -> 68.3 us (0.936)
  local copies, waits for them, and re-layouts: 3.22 us -> 0 us
  Pallas kernels: 69 us -> 67.5 us
    unnamed x7 -> x0, local copies, waits for them, and re-layouts: 3.22 us -> none
    pallas_call x1 -> x2, Pallas kernels: 69 us -> 67.5 us  [the longest x1 65.4 us: on_device(): pl.pallas_call(functools.partial(kernel, zn, gn), out_shape=(jax.ShapeDty...]
where the time goes in v4:
time: 68.3 us; the launch traced here: 68.1 us
  Pallas kernels  67.5 us (99%)
    pallas_call x1, Pallas kernels, on_device(): pl.pallas_call(functools.partial(kernel, zn, gn), out_shape=(jax.ShapeDty...  65.4 us
    pallas_call x1, Pallas kernels, on_device(): pl.pallas_call(functools.partial(finish, scale), out_shape=(jax.ShapeDtyp...  2.06 us

profile of v4, /device:TPU:1, one launch (start us, length us, event | category | flops | bytes accessed | tf_op | source)
XLA Modules:
  0.0 68.1 jit_solution(4601655965586571092)
XLA Ops:
  0.6 65.4 %shard_map.94 = (bf16[1024,128]{1,0:T(8,128)(2,1)}, bf16[1024,128]{1,0:T(8,128)(2,1)}, bf16[896,128]{1,0:T(8,128)(2,1)}) custom-call(bf16[1024,128]{1,0:T(8,128)(2,1)} %bitcast.10, s32[2,512]{1,0:T(2,128)} %occ_in.1, bf16[896,128]{1,0:T(8,128)(2,1)} %bitcast.14, bf16[1024,128]{1,0:T(8,128)(2,1)} %bitcast.11, s32[64]{0:T(128)} %bitcast.15, s32[64]{0:T(128)} %bitcast.16, ...), custom_call_target="tpu_custom_call" | custom-call | flops 704643072 | bytes 2000000 | tf_op jit(solution)/shard_map/pallas_call | solution.py:396
  66.1 2.1 %shard_map.95 = (bf16[1024,128]{1,0:T(8,128)(2,1)}, bf16[1024,128]{1,0:T(8,128)(2,1)}, f32[896,128]{1,0:T(8,128)}) custom-call(bf16[1024,128]{1,0:T(8,128)(2,1)} %get-tuple-element.9.act_in, bf16[1024,128]{1,0:T(8,128)(2,1)} %get-tuple-element.10.grad_in, bf16[896,128]{1,0:T(8,128)(2,1)} %get-tuple-element.11.wg_in), custom_call_target="tpu_custom_call" | custom-call | tf_op jit(solution)/shard_map/pallas_call | solution.py:464

commit v5 on v4

--- a/solution.py
+++ b/solution.py
@@ -62,7 +62,7 @@
         views[rows, 768:896] = shifted[...].astype(BF)
 
 
-ROW_OF = (0, 4, -1, 1, -2, 2, -3, 3)
+ROW_OF = (0, -1, 1, -2, 2, -3, 3, 4)
 PIECES = 3
 
 
@@ -73,8 +73,8 @@
     feat, occ, wcat, cot, count, sface, rface,
     mask, cube, ghost, shifted, views, wback, delta_t, run, prev, slot_face, slot_row, meta_out, meta_in, meta_far,
     faces_a, faces_b, rows_a, rows_b, got_a, got_b, up_a, down_a, up_b, down_b,
-    csend, crecv, zsend, zrecv, ygot, zgath, cgath, act, grad,
-    load_sems, out_sems, chain_a, chain_b, sems,
+    csend, crecv, zsend, zrecv, ygot, zgath, cgath, act, grad, inner,
+    load_sems, out_sems, chain_a, chain_b, sems_a, sems_b, sems,
 ):
     z = lax.axis_index("gx")
     me = lax.axis_index("gy")
@@ -97,8 +97,13 @@
     def xc_peer(k):
         return lax.rem(my_xc + k, xc_n)
 
-    def zx_peer(k):
-        return lax.rem(me_e + k, en)
+    def each_zx(body):
+        for dz in sorted(range(zn), key=lambda d: -min(d, zn - d)):
+            first = lax.rem(z + dz, zn) * XN
+            if dz:
+                repeat(0, XN, lambda x: body(first + x))
+            else:
+                repeat(1, XN, lambda k: body(first + lax.rem(my_x + k, XN)))
 
     def zx_device(e):
         return (e // XN, at(lax.rem(e, XN) * CN + my_c, my_y))
@@ -118,17 +123,6 @@
 
     def wait_for(ref, sem):
         pltpu.make_async_copy(ref, ref, sem).wait()
-
-    barrier = pltpu.get_barrier_semaphore()
-
-    def greet(to):
-        pl.semaphore_signal(barrier, inc=1, device_id=to, device_id_type=MESH)
-
-    repeat(1, YN, lambda k: greet((z, at(my_xc, wrap_y(k)))))
-    repeat(1, xc_n, lambda k: greet((z, at(xc_peer(k), my_y))))
-    repeat(1, xc_n, lambda k: greet((z, at(xc_peer(k), wrap_y(1)))))
-    repeat(1, xc_n, lambda k: greet((z, at(xc_peer(k), wrap_y(-1)))))
-    repeat(XN, en, lambda k: greet(zx_device(lax.rem(z * XN + k, en))))
 
     loads = [
         pltpu.make_async_copy(src, dst, load_sems.at[i])
@@ -137,7 +131,21 @@
              (cot_in, cot)]
         )
     ]
-    for load in loads:
+    for load in loads[:2]:
+        load.start()
+
+    barrier = pltpu.get_barrier_semaphore()
+
+    def greet(to):
+        pl.semaphore_signal(barrier, inc=1, device_id=to, device_id_type=MESH)
+
+    each_zx(lambda e: greet(zx_device(e)))
+    repeat(1, YN, lambda k: greet((z, at(my_xc, wrap_y(k)))))
+    repeat(1, xc_n, lambda k: greet((z, at(xc_peer(k), my_y))))
+    repeat(1, xc_n, lambda k: greet((z, at(xc_peer(k), wrap_y(1)))))
+    repeat(1, xc_n, lambda k: greet((z, at(xc_peer(k), wrap_y(-1)))))
+
+    for load in loads[2:]:
         load.start()
 
     diagonal = lax.broadcasted_iota(jnp.int32, (CH, CH), 0) == lax.broadcasted_iota(jnp.int32, (CH, CH), 1)
@@ -153,77 +161,69 @@
             mask[place : place + CH, :] = flags
             cube[place : place + CH, :] = jnp.where(flags > 0, feat[place : place + CH, :].astype(F32), 0.0)
     cut_faces(cube, faces_a)
-    loads[2].wait()
-    loads[3].wait()
-    loads[4].wait()
-
-    def fill_meta(y):
-        for xc in range(xc_n):
-            meta_out[y, xc] = sface[at(jnp.int32(xc), y)]
-            meta_out[y, xc_n + xc] = jnp.maximum(rface[at(jnp.int32(xc), y)], 0)
-
-    repeat(0, YN, fill_meta)
-
-    def start_exchange(faces, column, rows, got, up, down, chain, row_sems):
+    def start_chain(faces, up, down, chain):
         for p in range(PIECES):
-            part = pl.ds(p * 4, 4)
+            part = pl.ds(p * (FACES // PIECES), FACES // PIECES)
             send(faces.at[part], up[0].at[part], chain.at[0], chain.at[6 + p], (z, at(my_xc, wrap_y(1))))
-            send(faces.at[part], down[0].at[part], chain.at[3], chain.at[6 + 9 + p], (z, at(my_xc, wrap_y(-1))))
-
-        def pick(xc):
+            send(faces.at[part], down[0].at[part], chain.at[3], chain.at[6 + 3 * PIECES + p], (z, at(my_xc, wrap_y(-1))))
+
+    def start_row(faces, column, rows, got, up, down, chain, row_sems):
+        def ship(k):
+            xc = xc_peer(k)
             rows[xc, 0] = faces[meta_out[my_y, column + xc]]
-
-        repeat(0, xc_n, pick)
-
-        def ship_own(k):
-            xc = xc_peer(k)
             send(rows.at[xc, 0], got.at[my_xc, 0], row_sems.at[0], row_sems.at[1], (z, at(xc, my_y)))
 
-        repeat(1, xc_n, ship_own)
-        got[my_xc, 0] = rows[my_xc, 0]
+        repeat(1, xc_n, ship)
+        got[my_xc, 0] = faces[meta_out[my_y, column + my_xc]]
 
     def step_exchange(d, column, rows, got, up, down, chain, row_sems):
         for p in range(PIECES):
-            part = pl.ds(p * 4, 4)
-            wait_for(up[d - 1].at[part], chain.at[6 + (d - 1) * 3 + p])
+            part = pl.ds(p * (FACES // PIECES), FACES // PIECES)
+            wait_for(up[d - 1].at[part], chain.at[6 + (d - 1) * PIECES + p])
             if d < 3:
-                send(up[d - 1].at[part], up[d].at[part], chain.at[d], chain.at[6 + d * 3 + p],
+                send(up[d - 1].at[part], up[d].at[part], chain.at[d], chain.at[6 + d * PIECES + p],
                      (z, at(my_xc, wrap_y(1))))
-            wait_for(down[d - 1].at[part], chain.at[6 + 9 + (d - 1) * 3 + p])
+            wait_for(down[d - 1].at[part], chain.at[6 + (d + 2) * PIECES + p])
             if d < 3:
-                send(down[d - 1].at[part], down[d].at[part], chain.at[3 + d], chain.at[6 + 9 + d * 3 + p],
+                send(down[d - 1].at[part], down[d].at[part], chain.at[3 + d], chain.at[6 + (d + 3) * PIECES + p],
                      (z, at(my_xc, wrap_y(-1))))
+        if column == 0 and d == 1:
+            wait_for(meta_in.at[pl.ds(0, 6)], sems.at[5])
+            wait_for(meta_far.at[pl.ds(0, 2)], sems.at[19])
         low, high = wrap_y(-d), wrap_y(d)
 
-        def pick(xc):
-            rows[xc, 2 * d] = up[d - 1][meta_in[low, column + xc]]
-            rows[xc, 2 * d + 1] = down[d - 1][meta_in[high, column + xc]]
-
-        repeat(0, xc_n, pick)
-        pair = pl.ds(2 * d, 2)
-        if d == 3:
-            def pick_up(xc):
-                rows[xc, 1] = up[2][meta_far[low, column + xc]]
-                send(rows.at[xc, 1], got.at[my_xc, 1], row_sems.at[0], row_sems.at[1], (z, at(xc, wrap_y(1))))
-
-            def pick_down(xc):
-                rows[xc, 1] = down[2][meta_far[high, column + xc]]
-                send(rows.at[xc, 1], got.at[my_xc, 1], row_sems.at[0], row_sems.at[1], (z, at(xc, wrap_y(-1))))
-
-            repeat(0, xc_n // 2, pick_up)
-            repeat(xc_n // 2, xc_n, pick_down)
+        pair = pl.ds(2 * d - 1, 2)
+        landed = row_sems.at[1 + d]
 
         def ship(k):
             xc = xc_peer(k)
-            send(rows.at[xc, pair], got.at[my_xc, pair], row_sems.at[0], row_sems.at[1], (z, at(xc, my_y)))
-
+            rows[xc, 2 * d - 1] = up[d - 1][meta_in[low, column + xc]]
+            rows[xc, 2 * d] = down[d - 1][meta_in[high, column + xc]]
+            send(rows.at[xc, pair], got.at[my_xc, pair], row_sems.at[0], landed, (z, at(xc, my_y)))
+
+        def ship_up(xc):
+            rows[xc, 7] = up[2][meta_far[low, column + xc]]
+            send(rows.at[xc, 7], got.at[my_xc, 7], row_sems.at[0], landed, (z, at(xc, wrap_y(1))))
+
+        def ship_down(xc):
+            rows[xc, 7] = down[2][meta_far[high, column + xc]]
+            send(rows.at[xc, 7], got.at[my_xc, 7], row_sems.at[0], landed, (z, at(xc, wrap_y(-1))))
+
+        if d == 3:
+            repeat(0, xc_n // 2, ship_up)
+            repeat(xc_n // 2, xc_n, ship_down)
         repeat(1, xc_n, ship)
-        got[my_xc, pair] = rows[my_xc, pair]
+        got[my_xc, 2 * d - 1] = up[d - 1][meta_in[low, column + my_xc]]
+        got[my_xc, 2 * d] = down[d - 1][meta_in[high, column + my_xc]]
 
     remote_faces = (xc_n - 1) * 7 + xc_n
 
     def flat(ref):
         return ref.reshape(xc_n * 8, 64, CH).at[pl.ds(0, remote_faces)]
+
+    def wait_group(g, got, row_sems):
+        many = (xc_n - 1) * (2 if g else 1) + (xc_n if g == 3 else 0)
+        wait_for(got.reshape(xc_n * 8, 64, CH).at[pl.ds(0, many)], row_sems.at[1 + g])
 
     def drain(rows, up, down, chain, row_sems):
         for d in range(3):
@@ -231,29 +231,38 @@
             wait_for(down[d], chain.at[3 + d])
         wait_for(flat(rows), row_sems.at[0])
 
-    pl.semaphore_wait(barrier, (YN - 1) + 3 * (xc_n - 1) + (zn - 1) * XN)
-    sems_a, sems_b = sems.at[pl.ds(0, 2)], sems.at[pl.ds(2, 2)]
+    pl.semaphore_wait(barrier, (YN - 1) + 3 * (xc_n - 1) + (en - 1))
+    first = (rows_a, got_a, up_a, down_a, chain_a, sems_a)
+    second = (rows_b, got_b, up_b, down_b, chain_b, sems_b)
+    start_chain(faces_a, up_a, down_a, chain_a)
+    loads[2].wait()
+    loads[3].wait()
+    loads[4].wait()
+
+    def fill_meta(y):
+        for xc in range(xc_n):
+            meta_out[y, xc] = sface[at(jnp.int32(xc), y)]
+            meta_out[y, xc_n + xc] = jnp.maximum(rface[at(jnp.int32(xc), y)], 0)
+
+    repeat(0, YN, fill_meta)
+
     for d in (1, -1, 2, -2, 3, -3):
         y = wrap_y(d)
         send(meta_out.at[y], meta_in.at[my_y], sems.at[4], sems.at[5], (z, at(my_xc, y)))
     for d in (3, -3):
         send(meta_out.at[wrap_y(4)], meta_far.at[my_y], sems.at[18], sems.at[19], (z, at(my_xc, wrap_y(d))))
-    first = (rows_a, got_a, up_a, down_a, chain_a, sems_a)
-    second = (rows_b, got_b, up_b, down_b, chain_b, sems_b)
-    start_exchange(faces_a, 0, *first)
-
-    wait_for(meta_in.at[pl.ds(0, 6)], sems.at[5])
+    start_row(faces_a, 0, *first)
+
     step_exchange(1, 0, *first)
     step_exchange(2, 0, *first)
 
-    wait_for(meta_far.at[pl.ds(0, 2)], sems.at[19])
     step_exchange(3, 0, *first)
 
     def list_slots(xc):
         for s in range(8):
             p = at(xc, wrap_y(ROW_OF[s]))
-            slot_row[xc * 8 + s] = rface[p]
-            slot_face[xc * 8 + s] = jnp.where(count[p] > 0, sface[p], FACES)
+            slot_row[s * xc_n + xc] = rface[p]
+            slot_face[s * xc_n + xc] = jnp.where(count[p] > 0, sface[p], FACES)
 
     repeat(0, xc_n, list_slots)
 
@@ -277,10 +286,11 @@
         o = OPPOSITE[t]
         wback[t * CH : (t + 1) * CH, :] = wcat[o * CH : (o + 1) * CH, :].astype(F32).T.astype(BF)
 
-    wait_for(flat(got_a), sems_a.at[1])
+    for g in range(4):
+        wait_group(g, got_a, sems_a)
     for f in range(FACES):
         j = jnp.maximum(source[f], 0)
-        taken = got_a[j // 8, lax.rem(j, 8)].astype(F32)
+        taken = got_a[lax.rem(j, xc_n), j // xc_n].astype(F32)
         ghost[f] = jnp.where(source[f] >= 0, taken, 0.0)
 
     build_views(cube, ghost, shifted, views)
@@ -293,7 +303,8 @@
         delta = (cot[rows, :].astype(F32) * flags * sigma * (1.0 + preact * (1.0 - sigma))).astype(BF)
         cube[rows, :] = delta.astype(F32)
     cut_faces(cube, faces_b)
-    start_exchange(faces_b, xc_n, *second)
+    start_chain(faces_b, up_b, down_b, chain_b)
+    start_row(faces_b, xc_n, *second)
     store_act = pltpu.make_async_copy(act, act_out, out_sems.at[0])
     store_act.start()
 
@@ -316,47 +327,67 @@
     def piece_of(ref, e):
         return ref.at[pl.ds(pl.multiple_of(e * piece, 16), piece)]
 
-    def scatter(k):
-        e = zx_peer(k)
+    def scatter(e):
         send(piece_of(zsend, e), zrecv.at[me_e], sems.at[8], sems.at[9], zx_device(e))
 
-    repeat(1, en, scatter)
+    each_zx(scatter)
     zrecv[me_e] = piece_of(zsend, me_e)[...]
     step_exchange(1, xc_n, *second)
+
+    ghost[...] = jnp.zeros(ghost.shape, F32)
+    build_views(cube, ghost, shifted, views)
+    for b in range(2 * NB):
+        rows = slice(b * VOX // 2, (b + 1) * VOX // 2)
+        inner[rows, :] = product(views[rows, :], wback[...])
+
+    run[0] = jnp.zeros((64, CH), F32)
+
+    def add_up(g):
+        wait_group(g, got_b, sems_b)
+        for s in ((0,), (1, 2), (3, 4), (5, 6, 7))[g]:
+            def add_one(xc, s=s):
+                run[s * xc_n + xc + 1] = run[prev[s * xc_n + xc]] + got_b[xc, s].astype(F32)
+
+            repeat(0, xc_n, add_one)
+
     step_exchange(2, xc_n, *second)
+    add_up(0)
     wait_for(zrecv.at[pl.ds(0, en - 1)], sems.at[9])
     ygot[my_y] = jnp.sum(zrecv[...].astype(F32), axis=0)
     repeat(1, YN, lambda k: send(
         ygot.at[my_y], ygot.at[my_y], sems.at[12], sems.at[13], (z, at(my_xc, wrap_y(k)))))
     step_exchange(3, xc_n, *second)
+    add_up(1)
     wait_for(ygot.at[pl.ds(0, YN - 1)], sems.at[13])
     total = ygot[0]
     for k in range(1, YN):
         total = total + ygot[k]
     mine = piece_of(zgath, me_e)
     mine[...] = total.astype(BF)
-    repeat(1, en, lambda k: send(mine, mine, sems.at[14], sems.at[15], zx_device(zx_peer(k))))
-
-    wait_for(flat(got_b), sems_b.at[1])
-    run[0] = jnp.zeros((64, CH), F32)
-
-    def add_up(xc):
-        for s in range(8):
-            j = xc * 8 + s
-            run[j + 1] = run[prev[j]] + got_b[xc, s].astype(F32)
-
-    repeat(0, xc_n, add_up)
-    for f in range(FACES):
-        ghost[f] = run[last[f]]
+    each_zx(lambda e: send(mine, mine, sems.at[14], sems.at[15], zx_device(e)))
+
+    add_up(2)
+    add_up(3)
+    for side in range(6):
+        faces = jnp.concatenate([run[last[b * 6 + side]] for b in range(NB)], axis=0).astype(BF)
+        layers = product(faces, wback[(1 + side) * CH : (2 + side) * CH, :])
+        for b in range(NB):
+            base = b * VOX
+            layer = layers[b * 64 : (b + 1) * 64, :]
+            if side < 2:
+                first_row = base + 448 * side
+                inner[first_row : first_row + 64, :] += layer
+            elif side < 4:
+                for x in range(8):
+                    first_row = base + x * 64 + 56 * (side - 2)
+                    inner[first_row : first_row + 8, :] += layer[x * 8 : (x + 1) * 8, :]
+            else:
+                inner[pl.ds(base + 7 * (side - 4), 64, stride=8), :] += layer
+    grad[...] = (mask[...] * inner[...]).astype(BF)
+    store_grad = pltpu.make_async_copy(grad, grad_out, out_sems.at[1])
+    store_grad.start()
     wait_for(zgath.at[pl.ds(0, (en - 1) * piece)], sems.at[15])
     send(zgath.at[pl.ds(0, half)], cgath, sems.at[16], sems.at[17], twin)
-    build_views(cube, ghost, shifted, views)
-    for b in range(2 * NB):
-        rows = slice(b * VOX // 2, (b + 1) * VOX // 2)
-        grad[rows, :] = (mask[rows, :] * product(views[rows, :], wback[...])).astype(BF)
-
-    store_grad = pltpu.make_async_copy(grad, grad_out, out_sems.at[1])
-    store_grad.start()
     store_own = pltpu.make_async_copy(zgath.at[pl.ds(0, half)], half_of(wg_out, my_c), out_sems.at[2])
     store_own.start()
     wait_for(cgath, sems.at[17])
@@ -440,10 +471,13 @@
             pltpu.VMEM((half, CH), BF),
             pltpu.VMEM((ROWS, CH), BF),
             pltpu.VMEM((ROWS, CH), BF),
+            pltpu.VMEM((ROWS, CH), F32),
             pltpu.SemaphoreType.DMA((7,)),
             pltpu.SemaphoreType.DMA((4,)),
-            pltpu.SemaphoreType.DMA((24,)),
-            pltpu.SemaphoreType.DMA((24,)),
+            pltpu.SemaphoreType.DMA((6 + 6 * PIECES,)),
+            pltpu.SemaphoreType.DMA((6 + 6 * PIECES,)),
+            pltpu.SemaphoreType.DMA((5,)),
+            pltpu.SemaphoreType.DMA((5,)),
             pltpu.SemaphoreType.DMA((20,)),
         ],
         compiler_params=pltpu.CompilerParams(
@@ -468,8 +502,9 @@
             jax.ShapeDtypeStruct((ROWS, CH), BF),
             jax.ShapeDtypeStruct((TAPS * CH, CH), F32),
         ),
-        in_specs=[vmem, vmem, vmem],
-        out_specs=(vmem, vmem, vmem),
+        grid=(2,),
+        in_specs=[pl.BlockSpec((n, CH), lambda i: (i, 0)) for n in (512, 512, 448)],
+        out_specs=tuple(pl.BlockSpec((n, CH), lambda i: (i, 0)) for n in (512, 512, 448)),
         compiler_params=pltpu.CompilerParams(vmem_limit_bytes=62 * 1024 * 1024),
     )(activated, grad, weight_grad)
     return (

time: 68.3 us -> 68.3 us (level)
  no operation moved by 1% of the time
where the time goes in v5:
time: 68.3 us; the launch traced here: 68.2 us
  Pallas kernels  67.5 us (99%)
    pallas_call x1, Pallas kernels, on_device(): pl.pallas_call(functools.partial(kernel, zn, gn), out_shape=(jax.ShapeDty...  65.5 us
    pallas_call x1, Pallas kernels, on_device(): pl.pallas_call(functools.partial(finish, scale), out_shape=(jax.ShapeDtyp...  2.04 us

profile of v5, /device:TPU:1, one launch (start us, length us, event | category | flops | bytes accessed | tf_op | source)
XLA Modules:
  0.0 68.2 jit_solution(14378332072740171408)
XLA Ops:
  0.6 65.5 %shard_map.94 = (bf16[1024,128]{1,0:T(8,128)(2,1)}, bf16[1024,128]{1,0:T(8,128)(2,1)}, bf16[896,128]{1,0:T(8,128)(2,1)}) custom-call(bf16[1024,128]{1,0:T(8,128)(2,1)} %bitcast.10, s32[2,512]{1,0:T(2,128)} %occ_in.1, bf16[896,128]{1,0:T(8,128)(2,1)} %bitcast.14, bf16[1024,128]{1,0:T(8,128)(2,1)} %bitcast.11, s32[64]{0:T(128)} %bitcast.15, s32[64]{0:T(128)} %bitcast.16, ...), custom_call_target="tpu_custom_call" | custom-call | flops 704643072 | bytes 2000000 | tf_op jit(solution)/shard_map/pallas_call | solution.py:427
  66.1 2.0 %shard_map.95 = (bf16[1024,128]{1,0:T(8,128)(2,1)}, bf16[1024,128]{1,0:T(8,128)(2,1)}, f32[896,128]{1,0:T(8,128)}) custom-call(bf16[1024,128]{1,0:T(8,128)(2,1)} %get-tuple-element.9.act_in, bf16[1024,128]{1,0:T(8,128)(2,1)} %get-tuple-element.10.grad_in, bf16[896,128]{1,0:T(8,128)(2,1)} %get-tuple-element.11.wg_in), custom_call_target="tpu_custom_call" | custom-call | tf_op jit(solution)/shard_map/pallas_call | solution.py:498
